TPU v7x, 32 devices: a whole 2x2x4 slice. The times are simulated.
32 devices in a mesh: groups: 2 (over y), span: 4 (over z), head: 4 (over x, core).
Axes of the slice: x: 2, y: 2, z: 4, core: 2. Of those that a mesh axis runs over, the one named last changes fastest.
Arguments:
- query_rows: bfloat16 [2048, 6144], P(('groups', 'span', 'head')), parts along dimension 0, may hold values from -6 to 6
- key_rows: bfloat16 [2048, 1024], P(('groups', 'span', 'head')), parts along dimension 0, may hold values from -6 to 6
- value_rows: bfloat16 [2048, 1024], P(('groups', 'span', 'head')), parts along dimension 0, may hold values from -6 to 6
- frame_counts: int32 [16], P('groups'), parts along dimension 0, may hold values from 1 to 4, as said below
- noise_levels: int32 [16], P('groups'), parts along dimension 0, may hold values from 0 to 63
- span_mask: int32 [16, 8], P('groups'), parts along dimension 0, may hold values from 0 to 1, as said below
- level_gate: bfloat16 [64, 6144], P(None, 'head'), may hold values from 0.19921875 to 1.796875
Outputs:
- attended: bfloat16 [2048, 6144], P(('groups', 'span', 'head')), parts along dimension 0
There are 2 independent parts, one for each index of `groups`. A program takes and returns all parts, laid end to end along the dimension named above; an argument that names none is the same for every part. Nothing has to cross between parts.
Inputs may be any that keep to these rules, and one draw needn't show every extreme that they name: `frame_counts`: each span holds at least one frame, and some span holds exactly 4. span_mask[c, c] = 1 for every span, span_mask[c, e] = 0 for e > c, entries below the diagonal are 0 or 1.
All inputs are finite; a program needn't handle non-finite values.
Results may differ from a plain program's by a relative error of at most 0.0033.
Values may be sent and summed in bfloat16 or wider, within the bound.
A program may use at most 64 MiB of HBM per device.

v0:
```python
import math

import jax
import jax.numpy as jnp
from jax import lax
from jax.sharding import PartitionSpec as P

HD = 128
FRAME_TOK = 32
CT = 128
CH_DEV = 2


def attend(slot_state, query_block, key_piece, value_piece, usable, score_scale):
    run_max, run_sum, run_acc = slot_state
    scores = (
        jnp.einsum("qhgd,khd->hgqk", query_block, key_piece, preferred_element_type=jnp.float32)
        * score_scale
    )
    scores = jnp.where(usable[None, None, None, :], scores, -jnp.inf)
    new_max = jnp.maximum(run_max, jnp.max(scores, axis=3))
    weights = jnp.exp(scores - new_max[..., None])
    factor = jnp.exp(run_max - new_max)
    new_sum = factor * run_sum + jnp.sum(weights, axis=3)
    update = jnp.einsum(
        "hgqk,khd->qhgd",
        weights.astype(jnp.bfloat16),
        value_piece,
        preferred_element_type=jnp.float32,
    )
    new_acc = run_acc * jnp.transpose(factor, (2, 0, 1))[..., None] + update
    return (new_max, new_sum, new_acc)


def body(query_rows, key_rows, value_rows, frame_counts, noise_levels, span_mask, level_gate):
    q_local, k_local, v_local = (
        lax.all_to_all(query_rows, "head", split_axis=1, concat_axis=0, tiled=True),
        lax.all_to_all(key_rows, "head", split_axis=1, concat_axis=0, tiled=True),
        lax.all_to_all(value_rows, "head", split_axis=1, concat_axis=0, tiled=True),
    )
    span_devices = lax.axis_size("span")
    device_index = lax.axis_index("span")
    heads_dev = q_local.shape[1] // HD
    kv_dev = k_local.shape[1] // HD
    group_size = heads_dev // kv_dev
    score_scale = 1.0 / math.sqrt(HD)
    first_block = q_local[:CT]
    second_block = q_local[CT:]
    own_spans = jnp.stack([2 * device_index, 2 * device_index + 1])
    total_rows = CH_DEV * span_devices * CT
    position = jnp.arange(CT, dtype=jnp.int32)
    live_rows = position[None, :] < (frame_counts * FRAME_TOK)[:, None]
    live_flat = live_rows.reshape(-1)
    queries = jnp.stack([first_block, second_block]).reshape(2, CT, kv_dev, group_size, HD)
    allowed = []
    query_live = []
    gate_rows = []
    for member in range(2):
        mask_row = lax.dynamic_index_in_dim(span_mask, own_spans[member], 0, keepdims=False)
        allowed.append((jnp.repeat(mask_row, CT, total_repeat_length=total_rows) > 0) & live_flat)
        query_live.append(lax.dynamic_index_in_dim(live_rows, own_spans[member], 0, keepdims=False))
        level_index = lax.dynamic_index_in_dim(noise_levels, own_spans[member], 0, keepdims=False)
        gate_rows.append(
            lax.dynamic_index_in_dim(level_gate, level_index, 0, keepdims=False).astype(jnp.float32)
        )
    allowed = jnp.stack(allowed)

    def fold_step(running, kv_piece):
        key_piece, value_piece = kv_piece
        piece_rows = key_piece.shape[0]
        key_piece = key_piece.reshape(piece_rows, kv_dev, HD)
        value_piece = value_piece.reshape(piece_rows, kv_dev, HD)
        usable = lax.slice_in_dim(allowed, 0, piece_rows, axis=1)
        results = []
        for member in range(2):
            slot_state = (running[0][member], running[1][member], running[2][member])

            def compute(slot_state, member=member):
                return attend(
                    slot_state, queries[member], key_piece, value_piece, usable[member], score_scale
                )

            def keep_state(slot_state):
                return slot_state

            results.append(lax.cond(jnp.any(usable[member]), compute, keep_state, slot_state))
        return (
            jnp.stack([results[0][0], results[1][0]]),
            jnp.stack([results[0][1], results[1][1]]),
            jnp.stack([results[0][2], results[1][2]]),
        )

    initial = (
        jnp.full((2, kv_dev, group_size, CT), -1e30, jnp.float32),
        jnp.zeros((2, kv_dev, group_size, CT), jnp.float32),
        jnp.zeros((2, CT, kv_dev, group_size, HD), jnp.float32),
    )
    run_max, run_sum, run_acc = fold_step(
        initial,
        (
            lax.all_gather(k_local, "span", axis=0, tiled=True),
            lax.all_gather(v_local, "span", axis=0, tiled=True),
        ),
    )
    outputs = []
    for member in range(2):
        normed = run_acc[member] / jnp.transpose(run_sum[member], (2, 0, 1))[..., None]
        normed = normed.reshape(CT, heads_dev * HD) * gate_rows[member][None, :]
        outputs.append(
            jnp.where(query_live[member][:, None], normed, jnp.float32(0.0)).astype(jnp.bfloat16)
        )
    first_out = outputs[0]
    second_out = outputs[1]
    merged = jnp.concatenate([first_out, second_out], axis=0)
    return lax.all_to_all(merged, "head", split_axis=0, concat_axis=1, tiled=True)


def solution(mesh):
    placed = (
        P(("groups", "span", "head"), None),
        P(("groups", "span", "head"), None),
        P(("groups", "span", "head"), None),
        P("groups"),
        P("groups"),
        P("groups", None),
        P(None, "head"),
    )
    return jax.shard_map(
        body,
        mesh=mesh,
        in_specs=placed,
        out_specs=P(("groups", "span", "head"), None),
        check_vma=False,
    )
```

profile of v0, /device:TPU:0, one launch (start us, length us, event | category | flops | bytes accessed | tf_op | source)
XLA Modules:
  0.0 101.2 jit_solution(4558437299421896229)
XLA Ops:
  0.0 1.6 %copy.85 = bf16[8,4,8,256]{3,2,0,1:T(8,128)(2,1)} copy(bf16[8,4,8,256]{3,2,1,0:T(8,128)(2,1)} %bitcast.212) | data formatting | bytes 262144 | tf_op jit(solution)/shard_map/all_to_all | solution.py:38
  1.6 4.2 %all-to-all-start.1 = ((bf16[64,4,256]{2,0,1:T(8,128)(2,1)}), bf16[64,4,256]{2,0,1:T(8,128)(2,1)S(1)}, u32[]{:S(2)}, u32[]{:S(2)}) async-start(bf16[64,4,256]{2,0,1:T(8,128)(2,1)} %bitcast.201), calls=%async_computation.1 | async-start | bytes 262144 | tf_op jit(solution)/shard_map/all_to_all | solution.py:38
  5.8 0.7 broadcast_multiply_fusion
  6.4 1.5 %copy.84 = bf16[8,4,8,256]{3,2,0,1:T(8,128)(2,1)} copy(bf16[8,4,8,256]{3,2,1,0:T(8,128)(2,1)} %bitcast.213) | data formatting | bytes 262144 | tf_op jit(solution)/shard_map/all_to_all | solution.py:39
  8.0 0.8 fusion.52
  8.7 0.7 fusion.57
  9.5 1.0 all-to-all-done.1
  10.4 3.3 %all-to-all-start.2 = ((bf16[64,4,256]{2,0,1:T(8,128)(2,1)}), bf16[64,4,256]{2,0,1:T(8,128)(2,1)S(1)}, u32[]{:S(2)}, u32[]{:S(2)}) async-start(bf16[64,4,256]{2,0,1:T(8,128)(2,1)} %bitcast.200), calls=%async_computation.2 | async-start | bytes 262144 | tf_op jit(solution)/shard_map/all_to_all | solution.py:39
  13.7 10.7 %fusion.54 = (pred[]{:T(512)}, pred[1024]{0:T(1024)(128)(4,1)S(1)}, pred[]{:T(512)}, pred[1024]{0:T(1024)(128)(4,1)S(1)}) fusion(s32[8]{0:T(128)S(1)} %broadcast_multiply_fusion, s32[]{:T(128)} %bitcast.22, s32[]{:T(128)} %bitcast.21, s32[]{:T(128)} %bitcast.20, s32[]{:T(128)} %bitcast.19, s32[]{:T(128)} %bitcast.18, s32[]{:T(128)} %bitcast.17, s32[]{:T(128)} %bitcast.16, ...), kind=kLoop, calls=%fused_computation.79 | loop fusion | flops 38910 | bytes 2146 | tf_op jit(solution)/shard_map/reduce_or | solution.py:86
  24.4 2.1 %copy.83 = bf16[8,4,8,1536]{3,2,0,1:T(8,128)(2,1)} copy(bf16[8,4,8,1536]{3,2,1,0:T(8,128)(2,1)} %bitcast.207) | data formatting | bytes 1572864 | tf_op jit(solution)/shard_map/all_to_all | solution.py:37
  26.5 0.0 all-to-all-done.2
  26.5 3.5 %all-to-all-start = ((bf16[64,4,1536]{2,0,1:T(8,128)(2,1)}), bf16[64,4,1536]{2,0,1:T(8,128)(2,1)S(1)}, u32[]{:S(2)}, u32[]{:S(2)}) async-start(bf16[64,4,1536]{2,0,1:T(8,128)(2,1)} %bitcast.199), calls=%async_computation | async-start | bytes 1572864 | tf_op jit(solution)/shard_map/all_to_all | solution.py:37
  30.0 0.1 iota_compare_fusion
  30.1 1.4 %fusion.58 = (s32[1]{0:T(128)}, s32[1]{0:T(128)}) fusion(s32[8]{0:T(128)} %param.21, s32[]{:T(128)S(6)} %select_n.53, s32[]{:T(128)S(6)} %select_n.50), kind=kLoop, calls=%fused_computation.83 | loop fusion | bytes 24 | tf_op jit(solution)/shard_map/jit(dynamic_index_in_dim)/dynamic_slice | solution.py:62
  36.5 0.8 convert_reduce_fusion.1
  37.3 17.0 %all_gather.7 = bf16[1024,256]{1,0:T(8,128)(2,1)S(1)} all-gather(bf16[256,256]{1,0:T(8,128)(2,1)S(1)} %bitcast.209), channel_id=1, replica_groups=mesh['groups'=2,'span'=4,'head'=4] {'span'}, dimensions={0}, use_global_device_ids=true | all-gather | bytes 655360 | tf_op jit(solution)/shard_map/all_gather | solution.py:102
  54.3 1.0 copy.47
  55.3 15.5 %all_gather.6 = bf16[1024,256]{1,0:T(8,128)(2,1)S(1)} all-gather(bf16[256,256]{1,0:T(8,128)(2,1)S(1)} %bitcast.208), channel_id=1, replica_groups=mesh['groups'=2,'span'=4,'head'=4] {'span'}, dimensions={0}, use_global_device_ids=true | all-gather | bytes 655360 | tf_op jit(solution)/shard_map/all_gather | solution.py:101
  70.8 0.2 copy.45
  71.0 0.0 all-to-all-done
  71.0 0.1 fusion.56
  71.1 0.5 stack.10
  71.5 0.5 stack.9
  72.0 0.1 constant_dynamic-update-slice_fusion.1
  72.1 0.1 constant_dynamic-update-slice_fusion
  72.2 5.9 %conditional.2 = (f32[2,6,128]{2,1,0:T(8,128)S(1)}, f32[128,2,6,128]{0,3,2,1:T(8,128)S(1)}) conditional(s32[]{:T(128)} %convert_element_type.22, () %tuple.29, (pred[1024]{0:T(1024)(128)(4,1)S(1)}, bf16[2,128,2,6,128]{4,3,2,1,0:T(8,128)(2,1)S(1)}, bf16[1024,2,128]{0,2,1:T(8,128)(2,1)S(1)}, bf16[1024,2,128]{0,2,1:T(8,128)(2,1)}) %tuple.84), branch_computations={%region_1.3_spmd, %region_2.6_spmd} | conditional | flops 822809088 | bytes 26416172 | solution.py:86
  72.2 0.2 copy.48
  72.5 0.0 copy-start
  72.5 1.5 %bitcast_reduce_fusion = (f32[2,6,128]{2,1,0:T(8,128)S(1)}, f32[2,1024,128,6]{2,1,3,0:T(8,128)S(1)}) fusion(pred[1024]{0:T(1024)(128)(4,1)S(1)} %get-tuple-element.42, bf16[2,128,2,6,128]{4,1,3,2,0:T(8,128)(2,1)S(1)} %copy.48, bf16[1024,2,128]{0,2,1:T(8,128)(2,1)S(1)} %get-tuple-element.76), kind=kOutput, calls=%fused_computation.1 | convolution fusion | flops 407370240 | bytes 7216128 | tf_op jit(solution)/shard_map/cond/branch_1_fun/qhgd,khd->hgqk/dot_general | solution.py:17
  73.9 1.8 %fusion.2 = f32[2,6,128]{2,1,0:T(8,128)S(1)} fusion(f32[2,1024,128,6]{2,1,3,0:T(8,128)S(1)} %get-tuple-element.93, f32[2,6,128]{2,1,0:T(8,128)S(1)} %broadcast_maximum_fusion, pred[1024]{0:T(1024)(128)(4,1)S(1)} %get-tuple-element.42), kind=kLoop, calls=%fused_computation.5 | loop fusion | flops 6289920 | bytes 6304768 | tf_op jit(solution)/shard_map/cond/branch_1_fun/reduce_sum | solution.py:24
  75.7 0.0 copy-done
  75.8 2.1 %fusion.9 = f32[128,2,6,128]{3,0,2,1:T(8,128)S(1)} fusion(f32[2,1024,128,6]{2,1,3,0:T(8,128)S(1)} %get-tuple-element.93, f32[2,6,128]{2,1,0:T(8,128)S(1)} %broadcast_maximum_fusion, pred[1024]{0:T(1024)(128)(4,1)S(1)} %get-tuple-element.42, bf16[1024,2,128]{0,2,1:T(8,128)(2,1)S(1)} %copy-done, f32[128,2,6]{0,2,1:T(8,128)S(1)} %get-tuple-element.90), kind=kOutput, calls=%fused_computation.9 | convolution fusion | flops 409141248 | bytes 7615488 | tf_op jit(solution)/shard_map/cond/branch_1_fun/hgqk,khd->qhgd/dot_general | solution.py:25
  77.8 0.3 copy.73
  78.1 0.1 broadcast_divide_fusion.1
  78.2 6.0 %conditional.3 = (f32[2,6,128]{2,1,0:T(8,128)S(1)}, f32[128,2,6,128]{0,3,2,1:T(8,128)S(1)}) conditional(s32[]{:T(128)} %convert_element_type.24, () %tuple.31, (pred[1024]{0:T(1024)(128)(4,1)S(1)}, bf16[2,128,2,6,128]{4,3,2,1,0:T(8,128)(2,1)S(1)}, bf16[1024,2,128]{0,2,1:T(8,128)(2,1)S(1)}, bf16[1024,2,128]{0,2,1:T(8,128)(2,1)}) %tuple.85), branch_computations={%region_6.8_spmd, %region_7.11_spmd} | conditional | flops 822809088 | bytes 26416172 | solution.py:86
  78.4 0.2 copy.52
  78.6 0.0 copy-start.1
  78.6 1.5 %bitcast_reduce_fusion.1 = (f32[2,6,128]{2,1,0:T(8,128)S(1)}, f32[2,1024,128,6]{2,1,3,0:T(8,128)S(1)}) fusion(pred[1024]{0:T(1024)(128)(4,1)S(1)} %get-tuple-element.46, bf16[2,128,2,6,128]{4,1,3,2,0:T(8,128)(2,1)S(1)} %copy.52, bf16[1024,2,128]{0,2,1:T(8,128)(2,1)S(1)} %get-tuple-element.80), kind=kOutput, calls=%fused_computation.21 | convolution fusion | flops 407370240 | bytes 7216128 | tf_op jit(solution)/shard_map/cond/branch_1_fun/qhgd,khd->hgqk/dot_general | solution.py:17
  80.1 1.8 %fusion.21 = f32[2,6,128]{2,1,0:T(8,128)S(1)} fusion(f32[2,1024,128,6]{2,1,3,0:T(8,128)S(1)} %get-tuple-element.97, f32[2,6,128]{2,1,0:T(8,128)S(1)} %broadcast_maximum_fusion.1, pred[1024]{0:T(1024)(128)(4,1)S(1)} %get-tuple-element.46), kind=kLoop, calls=%fused_computation.25 | loop fusion | flops 6289920 | bytes 6304768 | tf_op jit(solution)/shard_map/cond/branch_1_fun/reduce_sum | solution.py:24
  81.9 2.1 %fusion.28 = f32[128,2,6,128]{3,0,2,1:T(8,128)S(1)} fusion(f32[2,1024,128,6]{2,1,3,0:T(8,128)S(1)} %get-tuple-element.97, f32[2,6,128]{2,1,0:T(8,128)S(1)} %broadcast_maximum_fusion.1, pred[1024]{0:T(1024)(128)(4,1)S(1)} %get-tuple-element.46, bf16[1024,2,128]{0,2,1:T(8,128)(2,1)S(1)} %copy-done.1, f32[128,2,6]{0,2,1:T(8,128)S(1)} %get-tuple-element.94), kind=kOutput, calls=%fused_computation.29 | convolution fusion | flops 409141248 | bytes 7615488 | tf_op jit(solution)/shard_map/cond/branch_1_fun/hgqk,khd->qhgd/dot_general | solution.py:25
  83.9 0.3 copy.75
  84.2 0.1 broadcast_divide_fusion
  84.3 0.3 fusion.41
  84.5 0.3 fusion.39
  84.8 0.1 pad_maximum_fusion
  84.9 0.3 copy.56
  85.2 15.1 %all_to_all.73 = bf16[4,64,1536]{2,1,0:T(8,128)(2,1)S(1)} all-to-all(bf16[4,64,1536]{2,1,0:T(8,128)(2,1)S(1)} %bitcast.205), channel_id=1, replica_groups=mesh['groups'=2,'span'=4,'head'=4] {'head'}, dimensions={0} | all-to-all | bytes 1572864 | tf_op jit(solution)/shard_map/all_to_all | solution.py:115
  100.3 0.9 copy.79
  (6 shorter events, 0.0 us)
Async XLA Ops:
  1.6 8.8 %all-to-all-start.1 = ((bf16[64,4,256]{2,0,1:T(8,128)(2,1)}), bf16[64,4,256]{2,0,1:T(8,128)(2,1)S(1)}, u32[]{:S(2)}, u32[]{:S(2)}) async-start(bf16[64,4,256]{2,0,1:T(8,128)(2,1)} %bitcast.201), calls=%async_computation.1 | async-start | bytes 262144 | tf_op jit(solution)/shard_map/all_to_all | solution.py:38
  10.4 16.1 %all-to-all-start.2 = ((bf16[64,4,256]{2,0,1:T(8,128)(2,1)}), bf16[64,4,256]{2,0,1:T(8,128)(2,1)S(1)}, u32[]{:S(2)}, u32[]{:S(2)}) async-start(bf16[64,4,256]{2,0,1:T(8,128)(2,1)} %bitcast.200), calls=%async_computation.2 | async-start | bytes 262144 | tf_op jit(solution)/shard_map/all_to_all | solution.py:39
  26.5 44.5 %all-to-all-start = ((bf16[64,4,1536]{2,0,1:T(8,128)(2,1)}), bf16[64,4,1536]{2,0,1:T(8,128)(2,1)S(1)}, u32[]{:S(2)}, u32[]{:S(2)}) async-start(bf16[64,4,1536]{2,0,1:T(8,128)(2,1)} %bitcast.199), calls=%async_computation | async-start | bytes 1572864 | tf_op jit(solution)/shard_map/all_to_all | solution.py:37
  72.5 3.3 %copy-start = (bf16[1024,2,128]{0,2,1:T(8,128)(2,1)S(1)}, bf16[1024,2,128]{0,2,1:T(8,128)(2,1)}, u32[]{:S(2)}) copy-start(bf16[1024,2,128]{0,2,1:T(8,128)(2,1)} %get-tuple-element.77) | copy-start | bytes 1572868 | tf_op jit(solution)/shard_map/cond
  78.6 3.3 %copy-start.1 = (bf16[1024,2,128]{0,2,1:T(8,128)(2,1)S(1)}, bf16[1024,2,128]{0,2,1:T(8,128)(2,1)}, u32[]{:S(2)}) copy-start(bf16[1024,2,128]{0,2,1:T(8,128)(2,1)} %get-tuple-element.81) | copy-start | bytes 1572868 | tf_op jit(solution)/shard_map/cond
where the time goes:
time: 102 us; the launch traced here: 101 us
  blocking collectives  47.6 us (47%)
  other arithmetic  16.6 us (16%)
  local copies, waits for them, and re-layouts  12.6 us (12%)
  starting transfers between devices  11 us (11%)
  matrix products  7.04 us (7%)
  between operations  5.14 us (5%)
    all_gather x1, blocking collectives, body(): lax.all_gather(v_local, 'span', axis=0, tiled=True)  17 us
    all_gather x1, blocking collectives, body(): lax.all_gather(k_local, 'span', axis=0, tiled=True)  15.5 us
    all_to_all x1, blocking collectives, body(): lax.all_to_all(merged, 'head', split_axis=0, concat_axis=1, tiled=True)  15.1 us
    reduce_or x1, other arithmetic, fold_step(): jnp.any(usable[member])  10.7 us
    all_to_all x1, starting transfers between devices, body(): lax.all_to_all(key_rows, 'head', split_axis=1, concat_axis=0, tiled=True)  4.21 us
    dot_general x2, matrix products, attend(): jnp.einsum('hgqk,khd->qhgd', weights.astype(jnp.bfloat16), value_piece, p...  4.1 us
    reduce_sum x2, other arithmetic, attend(): new_sum = factor * run_sum + jnp.sum(weights, axis=3)  3.54 us
    all_to_all x1, starting transfers between devices, body(): lax.all_to_all(query_rows, 'head', split_axis=1, concat_axis=0, tiled=True)  3.5 us
  transfers between devices with their start and end apart: 3, of which 1 were waited for; matrix products, arithmetic and copies ran while one was open for 20% of the time, Pallas kernels for 0%

commit v1 on v0

v1 whole, which is shorter than its diff:
```python
import functools
import math

import jax
import jax.numpy as jnp
from jax import lax
from jax.experimental import pallas as pl
from jax.experimental.pallas import tpu as pltpu
from jax.sharding import PartitionSpec as P

HD = 128
FRAME_TOK = 32
CT = 128
CORES = 2
MESH = pl.DeviceIdType.MESH
LOW = -1e30


def kernel(
    levels, peers,
    q_ref, k_ref, v_ref, frames_ref, noise_ref, mask_ref, gate_ref,
    out_ref,
    kbuf, vbuf, acc, top, gate_out, gate_in,
    recv_sem, up_sem, across_sem, sib_sem, gate_send, gate_recv,
):
    rows = q_ref.shape[0]
    kv_heads = k_ref.shape[1] // HD
    heads = q_ref.shape[1] // HD
    group = heads // kv_heads
    heads_dev = gate_ref.shape[1] // HD
    chips = peers // CORES
    level_rows = peers * rows
    level_spans = level_rows // CT
    factor = math.log2(math.e) / math.sqrt(HD)

    z = lax.axis_index("span")
    me = lax.axis_index("head")
    chip, core = me // CORES, me % CORES
    sibling = chip * CORES + (1 - core)
    bufs = (kbuf, vbuf)

    barrier = pltpu.get_barrier_semaphore()
    for step in range(1, peers):
        pl.semaphore_signal(
            barrier, inc=1, device_id={"head": (me + step) % peers}, device_id_type=MESH
        )

    @pl.when(z > 0)
    def _():
        pl.semaphore_signal(barrier, inc=1, device_id={"span": z - 1}, device_id_type=MESH)

    kbuf[z, me] = k_ref[...]
    vbuf[z, me] = v_ref[...]
    acc[...] = jnp.zeros_like(acc)
    top[...] = jnp.full_like(top, LOW)
    for i in range(level_spans):
        level_index = noise_ref[z * level_spans + i]
        pick = lax.broadcasted_iota(jnp.int32, (8, gate_ref.shape[0]), 1) == level_index
        picked = jnp.dot(
            pick.astype(jnp.bfloat16), gate_ref[...], preferred_element_type=jnp.float32
        )
        for n in range(heads_dev):
            gate_out[i, n : n + 1, :] = picked[0:1, n * HD : (n + 1) * HD]

    pl.semaphore_wait(barrier, peers - 1 + jnp.where(z < levels - 1, 1, 0))

    def copy(kv, level, slot, send_sem, target):
        return pltpu.make_async_remote_copy(
            src_ref=bufs[kv].at[level, slot],
            dst_ref=bufs[kv].at[level, slot],
            send_sem=send_sem,
            recv_sem=recv_sem.at[level, slot, kv],
            device_id=target,
            device_id_type=MESH,
        )

    def up(kv, level):
        return copy(kv, level, me, up_sem.at[level, kv], {"span": z + 1})

    def across(kv, level, step):
        other = (chip + step) % chips
        return copy(
            kv, level, me, across_sem.at[level, step - 1, kv], {"head": other * CORES + core}
        )

    def to_sibling(kv, level, step):
        slot = ((chip + step) % chips) * CORES + core
        return copy(kv, level, slot, sib_sem.at[level, step, kv], {"head": sibling})

    def wait_slot(kv, level, slot):
        copy(kv, level, slot, up_sem.at[level, kv], {"head": sibling}).wait_recv()

    def issue(kv, level):
        @pl.when(z < levels - 1)
        def _():
            up(kv, level).start()

        for step in range(1, chips):
            across(kv, level, step).start()
        to_sibling(kv, level, 0).start()

    def gate_copy(step):
        target = (me + step) % peers
        return pltpu.make_async_remote_copy(
            src_ref=gate_out.at[(target * rows) // CT],
            dst_ref=gate_in.at[me],
            send_sem=gate_send.at[step],
            recv_sem=gate_recv.at[me],
            device_id={"head": target},
            device_id_type=MESH,
        )

    for kv in range(2):
        issue(kv, z)
    for step in range(1, peers):
        gate_copy(step).start()

    token = me * rows
    span = z * level_spans + token // CT
    gate_in[me] = gate_out[token // CT]

    def fold(level):
        column = lax.broadcasted_iota(jnp.int32, (1, level_rows), 1)
        usable = column < 0
        for i in range(level_spans):
            key_span = level * level_spans + i
            limit = jnp.where(mask_ref[span, key_span] > 0, frames_ref[key_span] * FRAME_TOK, 0)
            usable = usable | ((column >= i * CT) & (column < i * CT + limit))
        bias = jnp.where(usable, jnp.float32(0.0), jnp.float32(LOW))
        ones = jnp.ones((level_rows, HD), jnp.bfloat16)

        def one_head(j, carry):
            lanes = pl.ds(pl.multiple_of(j * HD, HD), HD)
            queries = jnp.concatenate(
                [
                    q_ref[:, pl.ds(pl.multiple_of((j * group + g) * HD, HD), HD)]
                    for g in range(group)
                ],
                axis=0,
            )
            keys = kbuf[level, :, :, lanes].reshape(level_rows, HD)
            values = vbuf[level, :, :, lanes].reshape(level_rows, HD)
            scores = lax.dot_general(
                queries, keys, (((1,), (1,)), ((), ())), preferred_element_type=jnp.float32
            )
            scores = scores + bias
            old = top[j]
            new = jnp.maximum(old, jnp.max(scores, axis=1, keepdims=True))
            top[j] = new
            weights = jnp.exp2((scores - new[:, :1]) * factor).astype(jnp.bfloat16)
            update = jnp.dot(
                weights,
                jnp.concatenate([values, ones], axis=1),
                preferred_element_type=jnp.float32,
            )
            shrink = jnp.exp2((old - new) * factor)
            acc[j] = acc[j] * jnp.concatenate([shrink, shrink], axis=1) + update
            return carry

        lax.fori_loop(0, kv_heads, one_head, 0)

    def one_level(s, carry):
        level = z - s

        @pl.when(s < z)
        def _():
            for kv in range(2):
                wait_slot(kv, level - 1, me)
                issue(kv, level - 1)

        for kv in range(2):
            for step in range(1, chips):
                wait_slot(kv, level, ((chip + step) % chips) * CORES + core)
                to_sibling(kv, level, step).start()
        for kv in range(2):
            for step in range(chips):
                wait_slot(kv, level, ((chip + step) % chips) * CORES + 1 - core)
        fold(level)
        return carry

    lax.fori_loop(0, z + 1, one_level, 0)

    for step in range(1, peers):
        source = (me + step) % peers
        pltpu.make_async_remote_copy(
            src_ref=gate_out.at[0],
            dst_ref=gate_in.at[source],
            send_sem=gate_send.at[step],
            recv_sem=gate_recv.at[source],
            device_id={"head": source},
            device_id_type=MESH,
        ).wait_recv()

    position = token % CT + lax.broadcasted_iota(jnp.int32, (rows, HD), 0)
    live = position < frames_ref[span] * FRAME_TOK

    def finish(j, carry):
        for g in range(group):
            head = j * group + g
            part = slice(g * rows, (g + 1) * rows)
            gate = gate_in[head // heads_dev, pl.ds(head % heads_dev, 1), :]
            ratio = acc[j, part, :HD] / acc[j, part, HD:]
            out_ref[:, pl.ds(pl.multiple_of(head * HD, HD), HD)] = jnp.where(
                live, ratio * gate, jnp.float32(0.0)
            ).astype(out_ref.dtype)
        return carry

    lax.fori_loop(0, kv_heads, finish, 0)

    def drain(s, carry):
        level = z - s
        for kv in range(2):
            @pl.when(z < levels - 1)
            def _():
                up(kv, level).wait_send()

            for step in range(1, chips):
                across(kv, level, step).wait_send()
            for step in range(chips):
                to_sibling(kv, level, step).wait_send()
        return carry

    lax.fori_loop(0, z + 1, drain, 0)
    for step in range(1, peers):
        gate_copy(step).wait_send()


def body(levels, peers, q, k, v, frames, noise, mask, gate):
    rows, kv_width = k.shape
    kv_heads = kv_width // HD
    group_rows = q.shape[1] // kv_width * rows
    chips = peers // CORES
    level_spans = peers * rows // CT
    gate_rows = -(-(gate.shape[1] // HD) // 8) * 8
    vmem = pl.BlockSpec(memory_space=pltpu.VMEM)
    smem = pl.BlockSpec(memory_space=pltpu.SMEM)
    pairs = q.shape[0] * q.shape[1] // HD * levels * peers * rows
    return pl.pallas_call(
        functools.partial(kernel, levels, peers),
        out_shape=jax.ShapeDtypeStruct(q.shape, q.dtype),
        in_specs=[vmem, vmem, vmem, smem, smem, smem, vmem],
        out_specs=vmem,
        scratch_shapes=[
            pltpu.VMEM((levels, peers, rows, kv_width), k.dtype),
            pltpu.VMEM((levels, peers, rows, kv_width), v.dtype),
            pltpu.VMEM((kv_heads, group_rows, 2 * HD), jnp.float32),
            pltpu.VMEM((kv_heads, group_rows, HD), jnp.float32),
            pltpu.VMEM((level_spans, gate_rows, HD), jnp.float32),
            pltpu.VMEM((peers, gate_rows, HD), jnp.float32),
            pltpu.SemaphoreType.DMA((levels, peers, 2)),
            pltpu.SemaphoreType.DMA((levels, 2)),
            pltpu.SemaphoreType.DMA((levels, max(chips - 1, 1), 2)),
            pltpu.SemaphoreType.DMA((levels, chips, 2)),
            pltpu.SemaphoreType.DMA((peers,)),
            pltpu.SemaphoreType.DMA((peers,)),
        ],
        compiler_params=pltpu.CompilerParams(
            collective_id=0, has_side_effects=True, vmem_limit_bytes=40 << 20
        ),
        cost_estimate=pl.CostEstimate(
            flops=pairs * HD * 4, bytes_accessed=4 * q.size, transcendentals=pairs
        ),
    )(q, k, v, frames, noise, mask, gate)


def solution(mesh):
    placed = (
        P(("groups", "span", "head"), None),
        P(("groups", "span", "head"), None),
        P(("groups", "span", "head"), None),
        P("groups"),
        P("groups"),
        P("groups", None),
        P(None, "head"),
    )
    return jax.shard_map(
        functools.partial(body, mesh.shape["span"], mesh.shape["head"]),
        mesh=mesh,
        in_specs=placed,
        out_specs=P(("groups", "span", "head"), None),
        check_vma=False,
    )
```

time: 102 us -> 46.2 us (0.45)
  the two profiles are of different devices: /device:TPU:0 before, /device:TPU:25 now
where the time goes in v1:
time: 46.2 us; the launch traced here: 45.7 us
  Pallas kernels  39 us (84%)
  local copies, waits for them, and re-layouts  6.74 us (15%)
    pallas_call x1, Pallas kernels, body(): pl.pallas_call(functools.partial(kernel, levels, peers), out_shape=jax.Sh...  39 us
    unnamed x15, local copies, waits for them, and re-layouts  6.74 us

profile of v1, /device:TPU:25, one launch (start us, length us, event | category | flops | bytes accessed | tf_op | source)
XLA Modules:
  0.0 45.7 jit_solution(3007438396840728622)
XLA Ops:
  0.0 0.0 copy-start
  0.0 1.1 %copy-done = bf16[64,6144]{1,0:T(8,128)(2,1)S(1)} copy-done((bf16[64,6144]{1,0:T(8,128)(2,1)S(1)}, bf16[64,6144]{1,0:T(8,128)(2,1)}, u32[]{:S(2)}) %copy-start) | copy-done | bytes 786456
  1.1 0.0 copy-start.1
  1.1 0.9 %copy-done.1 = bf16[64,1536]{1,0:T(8,128)(2,1)S(1)} copy-done((bf16[64,1536]{1,0:T(8,128)(2,1)S(1)}, bf16[64,1536]{1,0:T(8,128)(2,1)}, u32[]{:S(2)}) %copy-start.1) | copy-done | bytes 196632
  2.1 0.0 copy-start.2
  2.1 0.9 %copy-done.2 = bf16[64,1024]{1,0:T(8,128)(2,1)S(1)} copy-done((bf16[64,1024]{1,0:T(8,128)(2,1)S(1)}, bf16[64,1024]{1,0:T(8,128)(2,1)}, u32[]{:S(2)}) %copy-start.2) | copy-done | bytes 131096
  3.0 0.0 copy-start.3
  3.0 0.9 %copy-done.3 = bf16[64,1024]{1,0:T(8,128)(2,1)S(1)} copy-done((bf16[64,1024]{1,0:T(8,128)(2,1)S(1)}, bf16[64,1024]{1,0:T(8,128)(2,1)}, u32[]{:S(2)}) %copy-start.3) | copy-done | bytes 131096
  3.9 0.0 copy-start.4
  3.9 0.7 %copy-done.4 = s32[8,8]{1,0:T(8,128)S(1)} copy-done((s32[8,8]{1,0:T(8,128)S(1)}, s32[8,8]{1,0:T(8,128)}, u32[]{:S(2)}) %copy-start.4) | copy-done | bytes 280
  4.6 0.0 copy-start.5
  4.6 0.7 %copy-done.5 = s32[8]{0:T(128)S(1)} copy-done((s32[8]{0:T(128)S(1)}, s32[8]{0:T(128)}, u32[]{:S(2)}) %copy-start.5) | copy-done | bytes 56
  5.2 0.0 copy-start.6
  5.2 0.7 %copy-done.6 = s32[8]{0:T(128)S(1)} copy-done((s32[8]{0:T(128)S(1)}, s32[8]{0:T(128)}, u32[]{:S(2)}) %copy-start.6) | copy-done | bytes 56
  5.9 39.0 %shard_map.73 = bf16[64,6144]{1,0:T(8,128)(2,1)S(1)} custom-call(bf16[64,6144]{1,0:T(8,128)(2,1)S(1)} %copy-done, bf16[64,1024]{1,0:T(8,128)(2,1)S(1)} %copy-done.2, bf16[64,1024]{1,0:T(8,128)(2,1)S(1)} %copy-done.3, s32[8]{0:T(128)S(1)} %copy-done.5, s32[8]{0:T(128)S(1)} %copy-done.6, s32[8,8]{1,0:T(8,128)S(1)} %copy-done.4, bf16[64,1536]{1,0:T(8,128)(2,1)S(1)} %copy-done.1), custom_call_target="tpu_custom_call" | custom-call | flops 1610612736 | bytes 1572864 | tf_op jit(solution)/shard_map/pallas_call | solution.py:238
  44.8 0.9 %copy.9 = bf16[64,6144]{1,0:T(8,128)(2,1)} copy(bf16[64,6144]{1,0:T(8,128)(2,1)S(1)} %shard_map.73) | data formatting | bytes 1572864
Async XLA Ops:
  0.0 1.1 %copy-start = (bf16[64,6144]{1,0:T(8,128)(2,1)S(1)}, bf16[64,6144]{1,0:T(8,128)(2,1)}, u32[]{:S(2)}) copy-start(bf16[64,6144]{1,0:T(8,128)(2,1)} %q_ref.1) | copy-start | bytes 2359300
  1.1 0.9 %copy-start.1 = (bf16[64,1536]{1,0:T(8,128)(2,1)S(1)}, bf16[64,1536]{1,0:T(8,128)(2,1)}, u32[]{:S(2)}) copy-start(bf16[64,1536]{1,0:T(8,128)(2,1)} %gate_ref.1) | copy-start | bytes 589828
  2.1 0.9 %copy-start.2 = (bf16[64,1024]{1,0:T(8,128)(2,1)S(1)}, bf16[64,1024]{1,0:T(8,128)(2,1)}, u32[]{:S(2)}) copy-start(bf16[64,1024]{1,0:T(8,128)(2,1)} %k_ref.1) | copy-start | bytes 393220
  3.0 0.9 %copy-start.3 = (bf16[64,1024]{1,0:T(8,128)(2,1)S(1)}, bf16[64,1024]{1,0:T(8,128)(2,1)}, u32[]{:S(2)}) copy-start(bf16[64,1024]{1,0:T(8,128)(2,1)} %v_ref.1) | copy-start | bytes 393220
  3.9 0.7 %copy-start.4 = (s32[8,8]{1,0:T(8,128)S(1)}, s32[8,8]{1,0:T(8,128)}, u32[]{:S(2)}) copy-start(s32[8,8]{1,0:T(8,128)} %mask_ref.1) | copy-start | bytes 772
  4.6 0.7 %copy-start.5 = (s32[8]{0:T(128)S(1)}, s32[8]{0:T(128)}, u32[]{:S(2)}) copy-start(s32[8]{0:T(128)} %frames_ref.1) | copy-start | bytes 100
  5.2 0.7 %copy-start.6 = (s32[8]{0:T(128)S(1)}, s32[8]{0:T(128)}, u32[]{:S(2)}) copy-start(s32[8]{0:T(128)} %noise_ref.1) | copy-start | bytes 100

commit v2 on v1

v2 whole, which is shorter than its diff:
```python
import functools
import math

import jax
import jax.numpy as jnp
from jax import lax
from jax.experimental import pallas as pl
from jax.experimental.pallas import tpu as pltpu
from jax.sharding import PartitionSpec as P

HD = 128
FRAME_TOK = 32
CT = 128
CORES = 2
MESH = pl.DeviceIdType.MESH
LOW = -1e30


def kernel(
    levels, peers, units,
    q_hbm, k_hbm, v_hbm, frames_hbm, noise_hbm, mask_hbm, gate_hbm,
    out_ref,
    kv_buf, q_ref, gate_ref, frames_ref, noise_ref, mask_ref, acc, top, gate_out, gate_in,
    recv_sem, up_sem, across_sem, sib_sem, gate_send, gate_recv, own_sem, load_sem,
):
    rows, kv_width = k_hbm.shape
    kv_heads = kv_width // HD
    heads = q_hbm.shape[1] // HD
    group = heads // kv_heads
    heads_dev = gate_hbm.shape[1] // HD
    chips = peers // CORES
    level_rows = peers * rows
    level_spans = level_rows // CT
    unit_heads = kv_heads // units
    unit_width = unit_heads * HD
    factor = math.log2(math.e) / math.sqrt(HD)

    z = lax.axis_index("span")
    me = lax.axis_index("head")
    chip, core = me // CORES, me % CORES
    sibling = chip * CORES + (1 - core)

    barrier = pltpu.get_barrier_semaphore()
    for step in range(1, peers):
        pl.semaphore_signal(
            barrier, inc=1, device_id={"head": (me + step) % peers}, device_id_type=MESH
        )

    @pl.when(z > 0)
    def _():
        pl.semaphore_signal(barrier, inc=1, device_id={"span": z - 1}, device_id_type=MESH)

    def piece(kv, unit):
        return (k_hbm, v_hbm)[kv].at[:, pl.ds(unit * unit_width, unit_width)]

    loads = [
        pltpu.make_async_copy(source, target, load_sem.at[n])
        for n, (source, target) in enumerate(
            (
                (frames_hbm, frames_ref),
                (noise_hbm, noise_ref),
                (mask_hbm, mask_ref),
                (gate_hbm, gate_ref),
                (q_hbm, q_ref),
            )
        )
    ]
    for load in loads:
        load.start()
    own = [
        [
            pltpu.make_async_copy(piece(kv, u), kv_buf.at[z, u, me, kv], own_sem.at[u, kv])
            for kv in range(2)
        ]
        for u in range(units)
    ]
    for u in range(units):
        for kv in range(2):
            own[u][kv].start()

    pl.semaphore_wait(barrier, peers - 1 + jnp.where(z < levels - 1, 1, 0))

    def copy(level, unit, slot, send_sem, target, kv=None):
        place = kv_buf.at[level, unit, slot]
        return pltpu.make_async_remote_copy(
            src_ref=place if kv is None else piece(kv, unit),
            dst_ref=place if kv is None else place.at[kv],
            send_sem=send_sem,
            recv_sem=recv_sem.at[level, unit, slot],
            device_id=target,
            device_id_type=MESH,
        )

    def up(level, unit, kv=None):
        return copy(level, unit, me, up_sem.at[level, unit], {"span": z + 1}, kv)

    def across(level, unit, step, kv=None):
        other = (chip + step) % chips
        return copy(
            level, unit, me, across_sem.at[level, unit, step - 1],
            {"head": other * CORES + core}, kv,
        )

    def to_sibling(level, unit, step, kv=None):
        slot = ((chip + step) % chips) * CORES + core
        return copy(level, unit, slot, sib_sem.at[level, unit, step], {"head": sibling}, kv)

    def wait_slot(level, unit, slot):
        copy(level, unit, slot, up_sem.at[level, unit], {"head": sibling}).wait_recv()

    def issue(level, unit, kv=None):
        @pl.when(z < levels - 1)
        def _():
            up(level, unit, kv).start()

        for step in range(1, chips):
            across(level, unit, step, kv).start()
        to_sibling(level, unit, 0, kv).start()

    def gate_copy(step):
        target = (me + step) % peers
        return pltpu.make_async_remote_copy(
            src_ref=gate_out.at[(target * rows) // CT],
            dst_ref=gate_in.at[me],
            send_sem=gate_send.at[step],
            recv_sem=gate_recv.at[me],
            device_id={"head": target},
            device_id_type=MESH,
        )

    for u in range(units):
        for kv in range(2):
            issue(z, u, kv)

    acc[...] = jnp.zeros_like(acc)
    top[...] = jnp.full_like(top, LOW)
    for load in loads:
        load.wait()
    for i in range(level_spans):
        level_index = noise_ref[z * level_spans + i]
        pick = lax.broadcasted_iota(jnp.int32, (8, gate_ref.shape[0]), 1) == level_index
        picked = jnp.dot(
            pick.astype(jnp.bfloat16), gate_ref[...], preferred_element_type=jnp.float32
        )
        for n in range(heads_dev):
            gate_out[i, n : n + 1, :] = picked[0:1, n * HD : (n + 1) * HD]
    for step in range(1, peers):
        gate_copy(step).start()

    token = me * rows
    span = z * level_spans + token // CT
    gate_in[me] = gate_out[token // CT]
    for u in range(units):
        for kv in range(2):
            own[u][kv].wait()

    def fold(level, unit):
        column = lax.broadcasted_iota(jnp.int32, (1, level_rows), 1)
        usable = column < 0
        for i in range(level_spans):
            key_span = level * level_spans + i
            limit = jnp.where(mask_ref[span, key_span] > 0, frames_ref[key_span] * FRAME_TOK, 0)
            usable = usable | ((column >= i * CT) & (column < i * CT + limit))
        bias = jnp.where(usable, jnp.float32(0.0), jnp.float32(LOW))
        ones = jnp.ones((level_rows, HD), jnp.bfloat16)

        for n in range(unit_heads):
            j = unit * unit_heads + n
            lanes = slice(n * HD, (n + 1) * HD)
            queries = jnp.concatenate(
                [
                    q_ref[:, (j * group + g) * HD : (j * group + g + 1) * HD]
                    for g in range(group)
                ],
                axis=0,
            )
            keys = kv_buf[level, unit, :, 0, :, lanes].reshape(level_rows, HD)
            values = kv_buf[level, unit, :, 1, :, lanes].reshape(level_rows, HD)
            scores = lax.dot_general(
                queries, keys, (((1,), (1,)), ((), ())), preferred_element_type=jnp.float32
            )
            scores = scores + bias
            old = top[j]
            new = jnp.maximum(old, jnp.max(scores, axis=1, keepdims=True))
            top[j] = new
            weights = jnp.exp2((scores - new[:, :1]) * factor).astype(jnp.bfloat16)
            update = jnp.dot(
                weights,
                jnp.concatenate([values, ones], axis=1),
                preferred_element_type=jnp.float32,
            )
            shrink = jnp.exp2((old - new) * factor)
            acc[j] = acc[j] * jnp.concatenate([shrink, shrink], axis=1) + update

    def forward(level, unit):
        for step in range(1, chips):
            wait_slot(level, unit, ((chip + step) % chips) * CORES + core)
            to_sibling(level, unit, step).start()

    forward(z, 0)

    def one_level(s, carry):
        level = z - s
        for u in range(units):
            ahead, ahead_unit = (u + 2) // units, (u + 2) % units

            @pl.when((s >= 1) if ahead == 0 else (s + ahead <= z))
            def _():
                wait_slot(level - ahead, ahead_unit, me)
                issue(level - ahead, ahead_unit)

            if u + 1 < units:
                forward(level, u + 1)
            else:
                @pl.when(s < z)
                def _():
                    forward(level - 1, 0)

            for step in range(chips):
                wait_slot(level, u, ((chip + step) % chips) * CORES + 1 - core)
            fold(level, u)
        return carry

    lax.fori_loop(0, z + 1, one_level, 0)

    for step in range(1, peers):
        source = (me + step) % peers
        pltpu.make_async_remote_copy(
            src_ref=gate_out.at[0],
            dst_ref=gate_in.at[source],
            send_sem=gate_send.at[step],
            recv_sem=gate_recv.at[source],
            device_id={"head": source},
            device_id_type=MESH,
        ).wait_recv()

    position = token % CT + lax.broadcasted_iota(jnp.int32, (rows, HD), 0)
    live = position < frames_ref[span] * FRAME_TOK

    for head in range(heads):
        j, g = head // group, head % group
        part = slice(g * rows, (g + 1) * rows)
        row = head % heads_dev
        gate = gate_in[head // heads_dev, row : row + 1, :]
        ratio = acc[j, part, :HD] / acc[j, part, HD:]
        out_ref[:, head * HD : (head + 1) * HD] = jnp.where(
            live, ratio * gate, jnp.float32(0.0)
        ).astype(out_ref.dtype)

    def drain(s, carry):
        level = z - s
        for u in range(units):
            @pl.when(z < levels - 1)
            def _():
                up(level, u).wait_send()

            for step in range(1, chips):
                across(level, u, step).wait_send()
            for step in range(chips):
                to_sibling(level, u, step).wait_send()
        return carry

    lax.fori_loop(0, z + 1, drain, 0)
    for step in range(1, peers):
        gate_copy(step).wait_send()


def body(levels, peers, q, k, v, frames, noise, mask, gate):
    rows, kv_width = k.shape
    kv_heads = kv_width // HD
    group_rows = q.shape[1] // kv_width * rows
    chips = peers // CORES
    units = kv_heads // 2
    level_spans = peers * rows // CT
    gate_rows = -(-(gate.shape[1] // HD) // 8) * 8
    hbm = pl.BlockSpec(memory_space=pltpu.HBM)
    pairs = q.shape[0] * q.shape[1] // HD * levels * peers * rows
    return pl.pallas_call(
        functools.partial(kernel, levels, peers, units),
        out_shape=jax.ShapeDtypeStruct(q.shape, q.dtype),
        in_specs=[hbm] * 7,
        out_specs=pl.BlockSpec(memory_space=pltpu.VMEM),
        scratch_shapes=[
            pltpu.VMEM((levels, units, peers, 2, rows, kv_width // units), k.dtype),
            pltpu.VMEM(q.shape, q.dtype),
            pltpu.VMEM(gate.shape, gate.dtype),
            pltpu.SMEM(frames.shape, frames.dtype),
            pltpu.SMEM(noise.shape, noise.dtype),
            pltpu.SMEM(mask.shape, mask.dtype),
            pltpu.VMEM((kv_heads, group_rows, 2 * HD), jnp.float32),
            pltpu.VMEM((kv_heads, group_rows, HD), jnp.float32),
            pltpu.VMEM((level_spans, gate_rows, HD), jnp.float32),
            pltpu.VMEM((peers, gate_rows, HD), jnp.float32),
            pltpu.SemaphoreType.DMA((levels, units, peers)),
            pltpu.SemaphoreType.DMA((levels, units)),
            pltpu.SemaphoreType.DMA((levels, units, max(chips - 1, 1))),
            pltpu.SemaphoreType.DMA((levels, units, chips)),
            pltpu.SemaphoreType.DMA((peers,)),
            pltpu.SemaphoreType.DMA((peers,)),
            pltpu.SemaphoreType.DMA((units, 2)),
            pltpu.SemaphoreType.DMA((5,)),
        ],
        compiler_params=pltpu.CompilerParams(
            collective_id=0, has_side_effects=True, vmem_limit_bytes=64 << 20
        ),
        cost_estimate=pl.CostEstimate(
            flops=pairs * HD * 4, bytes_accessed=4 * q.size, transcendentals=pairs
        ),
    )(q, k, v, frames, noise, mask, gate)


def solution(mesh):
    placed = (
        P(("groups", "span", "head"), None),
        P(("groups", "span", "head"), None),
        P(("groups", "span", "head"), None),
        P("groups"),
        P("groups"),
        P("groups", None),
        P(None, "head"),
    )
    return jax.shard_map(
        functools.partial(body, mesh.shape["span"], mesh.shape["head"]),
        mesh=mesh,
        in_specs=placed,
        out_specs=P(("groups", "span", "head"), None),
        check_vma=False,
    )
```

time: 46.2 us -> 42.7 us (0.924)
  local copies, waits for them, and re-layouts: 6.74 us -> 2.06 us
  Pallas kernels: 39 us -> 40.5 us
    unnamed x15 -> x1, local copies, waits for them, and re-layouts: 6.74 us -> 2.06 us
    pallas_call x1, Pallas kernels: 39 us -> 40.5 us  [body(): pl.pallas_call(functools.partial(kernel, levels, peers, units), out_shape...]
where the time goes in v2:
time: 42.7 us; the launch traced here: 42.6 us
  Pallas kernels  40.5 us (95%)
  local copies, waits for them, and re-layouts  2.06 us (5%)
    pallas_call x1, Pallas kernels, body(): pl.pallas_call(functools.partial(kernel, levels, peers, units), out_shape...  40.5 us
    unnamed x1, local copies, waits for them, and re-layouts  2.06 us

profile of v2, /device:TPU:25, one launch (start us, length us, event | category | flops | bytes accessed | tf_op | source)
XLA Modules:
  0.0 42.6 jit_solution(10834924152768331838)
XLA Ops:
  0.0 40.5 %shard_map.73 = bf16[64,6144]{1,0:T(8,128)(2,1)} custom-call(bf16[64,6144]{1,0:T(8,128)(2,1)} %q_hbm.1, bf16[64,1024]{1,0:T(8,128)(2,1)} %k_hbm.1, bf16[64,1024]{1,0:T(8,128)(2,1)} %v_hbm.1, s32[8]{0:T(128)} %frames_hbm.1, s32[8]{0:T(128)} %noise_hbm.1, s32[8,8]{1,0:T(8,128)} %mask_hbm.1, bf16[64,1536]{1,0:T(8,128)(2,1)} %gate_hbm.1), custom_call_target="tpu_custom_call" | custom-call | flops 1610612736 | bytes 1572864 | tf_op jit(solution)/shard_map/pallas_call | solution.py:278
  40.5 2.1 %copy.9 = bf16[64,6144]{1,0:T(8,128)(2,1)} copy(bf16[64,6144]{1,0:T(8,128)(2,1)} %shard_map.73) | data formatting | bytes 1572864

commit v3 on v2

v3 whole, which is shorter than its diff:
```python
import functools
import math

import jax
import jax.numpy as jnp
from jax import lax
from jax.experimental import pallas as pl
from jax.experimental.pallas import tpu as pltpu
from jax.sharding import PartitionSpec as P

HD = 128
FRAME_TOK = 32
CT = 128
CORES = 2
MESH = pl.DeviceIdType.MESH
LOW = -1e30


def kernel(
    levels, peers, units,
    q_hbm, k_hbm, v_hbm, frames_hbm, noise_hbm, mask_hbm, gate_hbm,
    out_hbm,
    kv_buf, q_ref, stage, gate_ref, frames_ref, noise_ref, mask_ref, acc, top, gate_out, gate_in,
    recv_sem, first_sem, up_sem, across_sem, gate_send, gate_recv, own_sem, load_sem,
    q_send, q_recv, out_send, out_recv, out_sem,
):
    rows, kv_width = k_hbm.shape
    kv_heads = kv_width // HD // CORES
    heads = q_hbm.shape[1] // HD // CORES
    group = heads // kv_heads
    heads_dev = gate_hbm.shape[1] // HD
    chips = peers // CORES
    chip_rows = CORES * rows
    level_rows = peers * rows
    level_spans = level_rows // CT
    unit_heads = kv_heads // units
    unit_width = unit_heads * HD
    factor = math.log2(math.e) / math.sqrt(HD)

    z = lax.axis_index("span")
    me = lax.axis_index("head")
    chip, core = me // CORES, me % CORES
    sibling = chip * CORES + (1 - core)

    barrier = pltpu.get_barrier_semaphore()
    for step in range(1, peers):
        pl.semaphore_signal(
            barrier, inc=1, device_id={"head": (me + step) % peers}, device_id_type=MESH
        )

    @pl.when(z > 0)
    def _():
        for other in (me, sibling):
            pl.semaphore_signal(
                barrier, inc=1, device_id={"span": z - 1, "head": other}, device_id_type=MESH
            )

    def lanes_of(owner, unit, width):
        start = (owner * units + unit) * width
        return pl.ds(pl.multiple_of(start, width), width)

    def piece(kv, owner, unit):
        return (k_hbm, v_hbm)[kv].at[:, lanes_of(owner, unit, unit_width)]

    def place(level, unit, slot, kv):
        return kv_buf.at[level, unit, slot, kv, core]

    def half(ref, owner):
        return ref.at[:, pl.ds(pl.multiple_of(owner * heads * HD, heads * HD), heads * HD)]

    loads = [
        pltpu.make_async_copy(source, target, load_sem.at[n])
        for n, (source, target) in enumerate(
            (
                (frames_hbm, frames_ref),
                (noise_hbm, noise_ref),
                (mask_hbm, mask_ref),
                (gate_hbm, gate_ref),
                (half(q_hbm, core), q_ref.at[core]),
            )
        )
    ]
    for load in loads:
        load.start()
    own = [
        pltpu.make_async_copy(piece(kv, core, u), place(z, u, chip, kv), own_sem.at[u, kv])
        for u in range(units)
        for kv in range(2)
    ]
    for load in own:
        load.start()

    pl.semaphore_wait(barrier, peers - 1 + jnp.where(z < levels - 1, CORES, 0))

    def send(source, target, send_sem, arrive_sem, device):
        return pltpu.make_async_remote_copy(
            src_ref=source,
            dst_ref=target,
            send_sem=send_sem,
            recv_sem=arrive_sem,
            device_id=device,
            device_id_type=MESH,
        )

    def first(unit, kv, turn, hop):
        owner = core if turn == 0 else 1 - core
        target = place(z, unit, chip, kv)
        if hop == "up":
            device = {"span": z + 1, "head": chip * CORES + owner}
            index = 0
        else:
            device = {"head": ((chip + hop) % chips) * CORES + owner}
            index = 1 + hop
        return send(
            piece(kv, owner, unit), target, first_sem.at[unit, kv, turn, index],
            recv_sem.at[z, unit, chip], device,
        )

    def first_copies(unit, turn):
        hops = list(range(1, chips)) + ([0] if turn else [])
        return [first(unit, kv, turn, hop) for hop in hops for kv in range(2)]

    def first_up(unit, turn):
        return [first(unit, kv, turn, "up") for kv in range(2)]

    def up(level, unit):
        slot = kv_buf.at[level, unit, chip]
        return send(
            slot, slot, up_sem.at[level, unit], recv_sem.at[level, unit, chip], {"span": z + 1}
        )

    def across(level, unit, step):
        slot = kv_buf.at[level, unit, chip]
        return send(
            slot, slot, across_sem.at[level, unit, step - 1], recv_sem.at[level, unit, chip],
            {"head": ((chip + step) % chips) * CORES + core},
        )

    def wait_slot(level, unit, slot):
        whole = kv_buf.at[level, unit, slot]
        send(
            whole, whole, up_sem.at[level, unit], recv_sem.at[level, unit, slot],
            {"head": sibling},
        ).wait_recv()

    def wait_sibling(unit):
        rest = kv_buf.at[z, unit, chip, :, 1 - core]
        send(
            rest, rest, up_sem.at[z, unit], recv_sem.at[z, unit, chip], {"head": sibling}
        ).wait_recv()

    def issue(level, unit):
        @pl.when(z < levels - 1)
        def _():
            up(level, unit).start()

        for step in range(1, chips):
            across(level, unit, step).start()

    swap = send(
        half(q_hbm, 1 - core), q_ref.at[core], q_send.at[0], q_recv.at[0], {"head": sibling}
    )

    def gate_copy(step):
        target = (me + step) % peers
        return send(
            gate_out.at[(target * rows) // CT], gate_in.at[me],
            gate_send.at[step], gate_recv.at[me], {"head": target},
        )

    for u in range(units):
        for turn in range(2):
            @pl.when(z < levels - 1)
            def _():
                for one in first_up(u, turn):
                    one.start()

            for one in first_copies(u, turn):
                one.start()
        if u == 0:
            swap.start()

    acc[...] = jnp.zeros_like(acc)
    top[...] = jnp.full_like(top, LOW)
    for load in loads:
        load.wait()
    for i in range(level_spans):
        level_index = noise_ref[z * level_spans + i]
        pick = lax.broadcasted_iota(jnp.int32, (8, gate_ref.shape[0]), 1) == level_index
        picked = jnp.dot(
            pick.astype(jnp.bfloat16), gate_ref[...], preferred_element_type=jnp.float32
        )
        for n in range(heads_dev):
            gate_out[i, n : n + 1, :] = picked[0:1, n * HD : (n + 1) * HD]
    for step in range(1, peers):
        gate_copy(step).start()

    token = chip * chip_rows
    span = z * level_spans + token // CT
    gate_in[me] = gate_out[token // CT]
    for load in own:
        load.wait()
    send(
        q_ref.at[1 - core], q_ref.at[1 - core], q_send.at[0], q_recv.at[0], {"head": sibling}
    ).wait_recv()
    for step in range(1, peers):
        source = (me + step) % peers
        send(
            gate_out.at[0], gate_in.at[source], gate_send.at[step], gate_recv.at[source],
            {"head": source},
        ).wait_recv()

    def fold(level, unit):
        column = lax.broadcasted_iota(jnp.int32, (1, level_rows), 1)
        usable = column < 0
        for i in range(level_spans):
            key_span = level * level_spans + i
            limit = jnp.where(mask_ref[span, key_span] > 0, frames_ref[key_span] * FRAME_TOK, 0)
            usable = usable | ((column >= i * CT) & (column < i * CT + limit))
        bias = jnp.where(usable, jnp.float32(0.0), jnp.float32(LOW))
        ones = jnp.ones((level_rows, HD), jnp.bfloat16)

        for n in range(unit_heads):
            j = unit * unit_heads + n
            lanes = slice(n * HD, (n + 1) * HD)
            queries = jnp.concatenate(
                [
                    q_ref[:, :, (j * group + g) * HD : (j * group + g + 1) * HD].reshape(
                        chip_rows, HD
                    )
                    for g in range(group)
                ],
                axis=0,
            )
            keys = kv_buf[level, unit, :, 0, :, :, lanes].reshape(level_rows, HD)
            values = kv_buf[level, unit, :, 1, :, :, lanes].reshape(level_rows, HD)
            scores = lax.dot_general(
                queries, keys, (((1,), (1,)), ((), ())), preferred_element_type=jnp.float32
            )
            scores = scores + bias
            old = top[j]
            new = jnp.maximum(old, jnp.max(scores, axis=1, keepdims=True))
            top[j] = new
            weights = jnp.exp2((scores - new[:, :1]) * factor).astype(jnp.bfloat16)
            update = jnp.dot(
                weights,
                jnp.concatenate([values, ones], axis=1),
                preferred_element_type=jnp.float32,
            )
            shrink = jnp.exp2((old - new) * factor)
            acc[j] = acc[j] * jnp.concatenate([shrink, shrink], axis=1) + update

    position = token % CT + lax.broadcasted_iota(jnp.int32, (chip_rows, HD), 0)
    live = position < frames_ref[span] * FRAME_TOK
    out_width = unit_width * group

    def out_lanes(owner, unit):
        return out_hbm.at[:, lanes_of(owner, unit, out_width)]

    def out_own(unit):
        return pltpu.make_async_copy(
            stage.at[unit, core], out_lanes(core, unit), out_sem.at[unit]
        )

    def out_swap(unit):
        return send(
            stage.at[unit, 1 - core], out_lanes(core, unit),
            out_send.at[unit], out_recv.at[unit], {"head": sibling},
        )

    def finish(unit):
        for n in range(unit_heads):
            j = unit * unit_heads + n
            for g in range(group):
                head = j * group + g
                part = slice(g * chip_rows, (g + 1) * chip_rows)
                row = head % heads_dev
                gate = gate_in[core * (peers // CORES) + head // heads_dev, row : row + 1, :]
                ratio = acc[j, part, :HD] / acc[j, part, HD:]
                done = jnp.where(live, ratio * gate, jnp.float32(0.0)).astype(stage.dtype)
                at = slice((n * group + g) * HD, (n * group + g + 1) * HD)
                stage[unit, :, :, at] = done.reshape(CORES, rows, HD)
        out_swap(unit).start()
        out_own(unit).start()

    def one_level(s, carry):
        level = z - s
        for u in range(units):
            ahead, ahead_unit = (u + 1) // units, (u + 1) % units

            @pl.when((s >= 1) if ahead == 0 else (s + ahead <= z))
            def _():
                wait_slot(level - ahead, ahead_unit, chip)
                issue(level - ahead, ahead_unit)

            @pl.when(s == 0)
            def _():
                wait_sibling(u)

            for step in range(1, chips):
                wait_slot(level, u, (chip + step) % chips)
            fold(level, u)

            @pl.when(s == z)
            def _():
                finish(u)
        return carry

    lax.fori_loop(0, z + 1, one_level, 0)

    for u in range(units):
        for turn in range(2):
            @pl.when(z < levels - 1)
            def _():
                for one in first_up(u, turn):
                    one.wait_send()

            for one in first_copies(u, turn):
                one.wait_send()

    def drain(s, carry):
        level = z - s
        for u in range(units):
            @pl.when(z < levels - 1)
            def _():
                up(level, u).wait_send()

            for step in range(1, chips):
                across(level, u, step).wait_send()
        return carry

    lax.fori_loop(1, z + 1, drain, 0)
    swap.wait_send()
    for step in range(1, peers):
        gate_copy(step).wait_send()
    for u in range(units):
        out_own(u).wait()
        out_swap(u).wait_send()
        send(
            stage.at[u, 1 - core], out_lanes(1 - core, u),
            out_send.at[u], out_recv.at[u], {"head": sibling},
        ).wait_recv()


def body(levels, peers, q, k, v, frames, noise, mask, gate):
    rows, kv_width = k.shape
    kv_heads = kv_width // HD // CORES
    group_rows = q.shape[1] // kv_width * rows * CORES
    chips = peers // CORES
    units = kv_heads // 2
    level_spans = peers * rows // CT
    gate_rows = -(-(gate.shape[1] // HD) // 8) * 8
    hbm = pl.BlockSpec(memory_space=pltpu.HBM)
    pairs = q.shape[0] * q.shape[1] // HD * levels * peers * rows
    unit_width = kv_width // CORES // units
    out_width = q.shape[1] // CORES // units
    return pl.pallas_call(
        functools.partial(kernel, levels, peers, units),
        out_shape=jax.ShapeDtypeStruct(q.shape, q.dtype),
        in_specs=[hbm] * 7,
        out_specs=hbm,
        scratch_shapes=[
            pltpu.VMEM((levels, units, chips, 2, CORES, rows, unit_width), k.dtype),
            pltpu.VMEM((CORES, rows, q.shape[1] // CORES), q.dtype),
            pltpu.VMEM((units, CORES, rows, out_width), q.dtype),
            pltpu.VMEM(gate.shape, gate.dtype),
            pltpu.SMEM(frames.shape, frames.dtype),
            pltpu.SMEM(noise.shape, noise.dtype),
            pltpu.SMEM(mask.shape, mask.dtype),
            pltpu.VMEM((kv_heads, group_rows, 2 * HD), jnp.float32),
            pltpu.VMEM((kv_heads, group_rows, HD), jnp.float32),
            pltpu.VMEM((level_spans, gate_rows, HD), jnp.float32),
            pltpu.VMEM((peers, gate_rows, HD), jnp.float32),
            pltpu.SemaphoreType.DMA((levels, units, chips)),
            pltpu.SemaphoreType.DMA((units, 2, 2, chips + 1)),
            pltpu.SemaphoreType.DMA((levels, units)),
            pltpu.SemaphoreType.DMA((levels, units, max(chips - 1, 1))),
            pltpu.SemaphoreType.DMA((peers,)),
            pltpu.SemaphoreType.DMA((peers,)),
            pltpu.SemaphoreType.DMA((units, 2)),
            pltpu.SemaphoreType.DMA((5,)),
            pltpu.SemaphoreType.DMA((1,)),
            pltpu.SemaphoreType.DMA((1,)),
            pltpu.SemaphoreType.DMA((units,)),
            pltpu.SemaphoreType.DMA((units,)),
            pltpu.SemaphoreType.DMA((units,)),
        ],
        compiler_params=pltpu.CompilerParams(
            collective_id=0, has_side_effects=True, vmem_limit_bytes=64 << 20
        ),
        cost_estimate=pl.CostEstimate(
            flops=pairs * HD * 4, bytes_accessed=4 * q.size, transcendentals=pairs
        ),
    )(q, k, v, frames, noise, mask, gate)


def solution(mesh):
    placed = (
        P(("groups", "span", "head"), None),
        P(("groups", "span", "head"), None),
        P(("groups", "span", "head"), None),
        P("groups"),
        P("groups"),
        P("groups", None),
        P(None, "head"),
    )
    return jax.shard_map(
        functools.partial(body, mesh.shape["span"], mesh.shape["head"]),
        mesh=mesh,
        in_specs=placed,
        out_specs=P(("groups", "span", "head"), None),
        check_vma=False,
    )
```

time: 42.7 us -> 37 us (0.87)
  Pallas kernels: 40.5 us -> 34.7 us
    pallas_call x1, Pallas kernels: 40.5 us -> 34.7 us  [body(): pl.pallas_call(functools.partial(kernel, levels, peers, units), out_shape...]
where the time goes in v3:
time: 37 us; the launch traced here: 36.8 us
  Pallas kernels  34.7 us (94%)
  local copies, waits for them, and re-layouts  2.06 us (6%)
    pallas_call x1, Pallas kernels, body(): pl.pallas_call(functools.partial(kernel, levels, peers, units), out_shape...  34.7 us
    unnamed x1, local copies, waits for them, and re-layouts  2.06 us

profile of v3, /device:TPU:25, one launch (start us, length us, event | category | flops | bytes accessed | tf_op | source)
XLA Modules:
  0.0 36.8 jit_solution(3915826209496847032)
XLA Ops:
  0.0 34.7 %shard_map.73 = bf16[64,6144]{1,0:T(8,128)(2,1)} custom-call(bf16[64,6144]{1,0:T(8,128)(2,1)} %q_hbm.1, bf16[64,1024]{1,0:T(8,128)(2,1)} %k_hbm.1, bf16[64,1024]{1,0:T(8,128)(2,1)} %v_hbm.1, s32[8]{0:T(128)} %frames_hbm.1, s32[8]{0:T(128)} %noise_hbm.1, s32[8,8]{1,0:T(8,128)} %mask_hbm.1, bf16[64,1536]{1,0:T(8,128)(2,1)} %gate_hbm.1), custom_call_target="tpu_custom_call" | custom-call | flops 1610612736 | bytes 1572864 | tf_op jit(solution)/shard_map/pallas_call | solution.py:357
  34.8 2.1 %copy.9 = bf16[64,6144]{1,0:T(8,128)(2,1)} copy(bf16[64,6144]{1,0:T(8,128)(2,1)} %shard_map.73) | data formatting | bytes 1572864

commit v4 on v3

--- a/solution.py
+++ b/solution.py
@@ -12,6 +12,7 @@
 FRAME_TOK = 32
 CT = 128
 CORES = 2
+PAIR = 2
 MESH = pl.DeviceIdType.MESH
 LOW = -1e30
 
@@ -35,6 +36,7 @@
     level_spans = level_rows // CT
     unit_heads = kv_heads // units
     unit_width = unit_heads * HD
+    tile = PAIR * chip_rows
     factor = math.log2(math.e) / math.sqrt(HD)
 
     z = lax.axis_index("span")
@@ -181,7 +183,8 @@
             swap.start()
 
     acc[...] = jnp.zeros_like(acc)
-    top[...] = jnp.full_like(top, LOW)
+    top[:, 0:1, :] = jnp.full((kv_heads, 1, top.shape[2]), LOW, jnp.float32)
+    top[:, 1:2, :] = jnp.zeros((kv_heads, 1, top.shape[2]), jnp.float32)
     for load in loads:
         load.wait()
     for i in range(level_spans):
@@ -211,44 +214,53 @@
         ).wait_recv()
 
     def fold(level, unit):
-        column = lax.broadcasted_iota(jnp.int32, (1, level_rows), 1)
-        usable = column < 0
+        row = lax.broadcasted_iota(jnp.int32, (level_rows, tile), 0)
+        usable = row < 0
         for i in range(level_spans):
             key_span = level * level_spans + i
             limit = jnp.where(mask_ref[span, key_span] > 0, frames_ref[key_span] * FRAME_TOK, 0)
-            usable = usable | ((column >= i * CT) & (column < i * CT + limit))
+            usable = usable | ((row >= i * CT) & (row < i * CT + limit))
         bias = jnp.where(usable, jnp.float32(0.0), jnp.float32(LOW))
-        ones = jnp.ones((level_rows, HD), jnp.bfloat16)
-
-        for n in range(unit_heads):
+
+        def score(n, t):
             j = unit * unit_heads + n
-            lanes = slice(n * HD, (n + 1) * HD)
             queries = jnp.concatenate(
                 [
                     q_ref[:, :, (j * group + g) * HD : (j * group + g + 1) * HD].reshape(
                         chip_rows, HD
                     )
-                    for g in range(group)
+                    for g in range(t * PAIR, (t + 1) * PAIR)
                 ],
                 axis=0,
             )
-            keys = kv_buf[level, unit, :, 0, :, :, lanes].reshape(level_rows, HD)
-            values = kv_buf[level, unit, :, 1, :, :, lanes].reshape(level_rows, HD)
-            scores = lax.dot_general(
-                queries, keys, (((1,), (1,)), ((), ())), preferred_element_type=jnp.float32
-            )
-            scores = scores + bias
-            old = top[j]
-            new = jnp.maximum(old, jnp.max(scores, axis=1, keepdims=True))
-            top[j] = new
-            weights = jnp.exp2((scores - new[:, :1]) * factor).astype(jnp.bfloat16)
+            keys = kv_buf[level, unit, :, 0, :, :, n * HD : (n + 1) * HD].reshape(level_rows, HD)
+            return lax.dot_general(
+                keys, queries, (((1,), (1,)), ((), ())), preferred_element_type=jnp.float32
+            )
+
+        steps = [(n, t) for n in range(unit_heads) for t in range(group // PAIR)]
+        ready = score(*steps[0])
+        for at, (n, t) in enumerate(steps):
+            scores = ready + bias
+            if at + 1 < len(steps):
+                ready = score(*steps[at + 1])
+            j = unit * unit_heads + n
+            lanes = slice(t * tile, (t + 1) * tile)
+            if t == 0:
+                values = kv_buf[level, unit, :, 1, :, :, n * HD : (n + 1) * HD]
+                values = values.reshape(level_rows, HD).T
+            old = top[j, 0:1, lanes]
+            new = jnp.maximum(old, jnp.max(scores, axis=0, keepdims=True))
+            top[j, 0:1, lanes] = new
+            weights = jnp.exp2((scores - new) * factor)
+            shrink = jnp.exp2((old - new) * factor)
+            top[j, 1:2, lanes] = top[j, 1:2, lanes] * shrink + jnp.sum(
+                weights, axis=0, keepdims=True
+            )
             update = jnp.dot(
-                weights,
-                jnp.concatenate([values, ones], axis=1),
-                preferred_element_type=jnp.float32,
-            )
-            shrink = jnp.exp2((old - new) * factor)
-            acc[j] = acc[j] * jnp.concatenate([shrink, shrink], axis=1) + update
+                values, weights.astype(jnp.bfloat16), preferred_element_type=jnp.float32
+            )
+            acc[j, :, lanes] = acc[j, :, lanes] * shrink + update
 
     position = token % CT + lax.broadcasted_iota(jnp.int32, (chip_rows, HD), 0)
     live = position < frames_ref[span] * FRAME_TOK
@@ -271,15 +283,17 @@
     def finish(unit):
         for n in range(unit_heads):
             j = unit * unit_heads + n
-            for g in range(group):
-                head = j * group + g
-                part = slice(g * chip_rows, (g + 1) * chip_rows)
-                row = head % heads_dev
-                gate = gate_in[core * (peers // CORES) + head // heads_dev, row : row + 1, :]
-                ratio = acc[j, part, :HD] / acc[j, part, HD:]
-                done = jnp.where(live, ratio * gate, jnp.float32(0.0)).astype(stage.dtype)
-                at = slice((n * group + g) * HD, (n * group + g + 1) * HD)
-                stage[unit, :, :, at] = done.reshape(CORES, rows, HD)
+            for t in range(group // PAIR):
+                lanes = slice(t * tile, (t + 1) * tile)
+                ratio = (acc[j, :, lanes] / top[j, 1:2, lanes]).T
+                for g in range(t * PAIR, (t + 1) * PAIR):
+                    head = j * group + g
+                    row = head % heads_dev
+                    gate = gate_in[core * (peers // CORES) + head // heads_dev, row : row + 1, :]
+                    part = ratio[(g - t * PAIR) * chip_rows : (g - t * PAIR + 1) * chip_rows]
+                    done = jnp.where(live, part * gate, jnp.float32(0.0)).astype(stage.dtype)
+                    at = slice((n * group + g) * HD, (n * group + g + 1) * HD)
+                    stage[unit, :, :, at] = done.reshape(CORES, rows, HD)
         out_swap(unit).start()
         out_own(unit).start()
 
@@ -367,8 +381,8 @@
             pltpu.SMEM(frames.shape, frames.dtype),
             pltpu.SMEM(noise.shape, noise.dtype),
             pltpu.SMEM(mask.shape, mask.dtype),
-            pltpu.VMEM((kv_heads, group_rows, 2 * HD), jnp.float32),
-            pltpu.VMEM((kv_heads, group_rows, HD), jnp.float32),
+            pltpu.VMEM((kv_heads, HD, group_rows), jnp.float32),
+            pltpu.VMEM((kv_heads, 2, group_rows), jnp.float32),
             pltpu.VMEM((level_spans, gate_rows, HD), jnp.float32),
             pltpu.VMEM((peers, gate_rows, HD), jnp.float32),
             pltpu.SemaphoreType.DMA((levels, units, chips)),

time: 37 us -> 38.9 us (1.051)
  Pallas kernels: 34.7 us -> 36.7 us
    pallas_call x1, Pallas kernels: 34.7 us -> 36.7 us  [body(): pl.pallas_call(functools.partial(kernel, levels, peers, units), out_shape...]
where the time goes in v4:
time: 38.9 us; the launch traced here: 38.8 us
  Pallas kernels  36.7 us (94%)
  local copies, waits for them, and re-layouts  2.06 us (5%)
    pallas_call x1, Pallas kernels, body(): pl.pallas_call(functools.partial(kernel, levels, peers, units), out_shape...  36.7 us
    unnamed x1, local copies, waits for them, and re-layouts  2.06 us

profile of v4, /device:TPU:25, one launch (start us, length us, event | category | flops | bytes accessed | tf_op | source)
XLA Modules:
  0.0 38.8 jit_solution(17923741510863924383)
XLA Ops:
  0.0 36.7 %shard_map.73 = bf16[64,6144]{1,0:T(8,128)(2,1)} custom-call(bf16[64,6144]{1,0:T(8,128)(2,1)} %q_hbm.1, bf16[64,1024]{1,0:T(8,128)(2,1)} %k_hbm.1, bf16[64,1024]{1,0:T(8,128)(2,1)} %v_hbm.1, s32[8]{0:T(128)} %frames_hbm.1, s32[8]{0:T(128)} %noise_hbm.1, s32[8,8]{1,0:T(8,128)} %mask_hbm.1, bf16[64,1536]{1,0:T(8,128)(2,1)} %gate_hbm.1), custom_call_target="tpu_custom_call" | custom-call | flops 1610612736 | bytes 1572864 | tf_op jit(solution)/shard_map/pallas_call | solution.py:371
  36.7 2.1 %copy.9 = bf16[64,6144]{1,0:T(8,128)(2,1)} copy(bf16[64,6144]{1,0:T(8,128)(2,1)} %shard_map.73) | data formatting | bytes 1572864

commit v5 on v3

--- a/solution.py
+++ b/solution.py
@@ -241,7 +241,8 @@
             old = top[j]
             new = jnp.maximum(old, jnp.max(scores, axis=1, keepdims=True))
             top[j] = new
-            weights = jnp.exp2((scores - new[:, :1]) * factor).astype(jnp.bfloat16)
+            wide = jnp.concatenate([new] * (level_rows // HD), axis=1)
+            weights = jnp.exp2((scores - wide) * factor).astype(jnp.bfloat16)
             update = jnp.dot(
                 weights,
                 jnp.concatenate([values, ones], axis=1),
@@ -286,12 +287,10 @@
     def one_level(s, carry):
         level = z - s
         for u in range(units):
-            ahead, ahead_unit = (u + 1) // units, (u + 1) % units
-
-            @pl.when((s >= 1) if ahead == 0 else (s + ahead <= z))
-            def _():
-                wait_slot(level - ahead, ahead_unit, chip)
-                issue(level - ahead, ahead_unit)
+            @pl.when(s < z)
+            def _():
+                wait_slot(level - 1, u, chip)
+                issue(level - 1, u)
 
             @pl.when(s == 0)
             def _():

time: 37 us -> 34.1 us (0.922)
  Pallas kernels: 34.7 us -> 31.9 us
    pallas_call x1, Pallas kernels: 34.7 us -> 31.9 us  [body(): pl.pallas_call(functools.partial(kernel, levels, peers, units), out_shape...]
where the time goes in v5:
time: 34.1 us; the launch traced here: 33.9 us
  Pallas kernels  31.9 us (94%)
  local copies, waits for them, and re-layouts  2.06 us (6%)
    pallas_call x1, Pallas kernels, body(): pl.pallas_call(functools.partial(kernel, levels, peers, units), out_shape...  31.9 us
    unnamed x1, local copies, waits for them, and re-layouts  2.06 us

profile of v5, /device:TPU:25, one launch (start us, length us, event | category | flops | bytes accessed | tf_op | source)
XLA Modules:
  0.0 33.9 jit_solution(976914788551271489)
XLA Ops:
  0.0 31.9 %shard_map.73 = bf16[64,6144]{1,0:T(8,128)(2,1)} custom-call(bf16[64,6144]{1,0:T(8,128)(2,1)} %q_hbm.1, bf16[64,1024]{1,0:T(8,128)(2,1)} %k_hbm.1, bf16[64,1024]{1,0:T(8,128)(2,1)} %v_hbm.1, s32[8]{0:T(128)} %frames_hbm.1, s32[8]{0:T(128)} %noise_hbm.1, s32[8,8]{1,0:T(8,128)} %mask_hbm.1, bf16[64,1536]{1,0:T(8,128)(2,1)} %gate_hbm.1), custom_call_target="tpu_custom_call" | custom-call | flops 1610612736 | bytes 1572864 | tf_op jit(solution)/shard_map/pallas_call | solution.py:356
  31.9 2.1 %copy.9 = bf16[64,6144]{1,0:T(8,128)(2,1)} copy(bf16[64,6144]{1,0:T(8,128)(2,1)} %shard_map.73) | data formatting | bytes 1572864

commit v6 on v5

--- a/solution.py
+++ b/solution.py
@@ -21,7 +21,7 @@
     q_hbm, k_hbm, v_hbm, frames_hbm, noise_hbm, mask_hbm, gate_hbm,
     out_hbm,
     kv_buf, q_ref, stage, gate_ref, frames_ref, noise_ref, mask_ref, acc, top, gate_out, gate_in,
-    recv_sem, first_sem, up_sem, across_sem, gate_send, gate_recv, own_sem, load_sem,
+    recv_sem, first_sem, up_sem, across_sem, other_sem, gate_send, gate_recv, own_sem, load_sem,
     q_send, q_recv, out_send, out_recv, out_sem,
 ):
     rows, kv_width = k_hbm.shape
@@ -149,13 +149,28 @@
             rest, rest, up_sem.at[z, unit], recv_sem.at[z, unit, chip], {"head": sibling}
         ).wait_recv()
 
+    def by_span(unit):
+        return chips == 2 and unit % 2 == 1
+
+    def up_other(unit, step):
+        slot = kv_buf.at[0, unit, (chip + step) % chips]
+        return send(
+            slot, slot, other_sem.at[unit, step - 1],
+            recv_sem.at[0, unit, (chip + step) % chips], {"span": z + 1},
+        )
+
+    def goes_across(level, unit):
+        return (level > 0) if by_span(unit) else (level >= 0)
+
     def issue(level, unit):
         @pl.when(z < levels - 1)
         def _():
             up(level, unit).start()
 
-        for step in range(1, chips):
-            across(level, unit, step).start()
+        @pl.when(goes_across(level, unit))
+        def _():
+            for step in range(1, chips):
+                across(level, unit, step).start()
 
     swap = send(
         half(q_hbm, 1 - core), q_ref.at[core], q_send.at[0], q_recv.at[0], {"head": sibling}
@@ -298,6 +313,11 @@
 
             for step in range(1, chips):
                 wait_slot(level, u, (chip + step) % chips)
+            if by_span(u):
+                @pl.when((s == z) & (z < levels - 1))
+                def _():
+                    for step in range(1, chips):
+                        up_other(u, step).start()
             fold(level, u)
 
             @pl.when(s == z)
@@ -324,11 +344,19 @@
             def _():
                 up(level, u).wait_send()
 
-            for step in range(1, chips):
-                across(level, u, step).wait_send()
+            @pl.when(goes_across(level, u))
+            def _():
+                for step in range(1, chips):
+                    across(level, u, step).wait_send()
         return carry
 
     lax.fori_loop(1, z + 1, drain, 0)
+    for u in range(units):
+        if by_span(u):
+            @pl.when(z < levels - 1)
+            def _():
+                for step in range(1, chips):
+                    up_other(u, step).wait_send()
     swap.wait_send()
     for step in range(1, peers):
         gate_copy(step).wait_send()
@@ -357,7 +385,7 @@
         functools.partial(kernel, levels, peers, units),
         out_shape=jax.ShapeDtypeStruct(q.shape, q.dtype),
         in_specs=[hbm] * 7,
-        out_specs=hbm,
+        out_specs=pl.BlockSpec(memory_space=pltpu.VMEM),
         scratch_shapes=[
             pltpu.VMEM((levels, units, chips, 2, CORES, rows, unit_width), k.dtype),
             pltpu.VMEM((CORES, rows, q.shape[1] // CORES), q.dtype),
@@ -374,6 +402,7 @@
             pltpu.SemaphoreType.DMA((units, 2, 2, chips + 1)),
             pltpu.SemaphoreType.DMA((levels, units)),
             pltpu.SemaphoreType.DMA((levels, units, max(chips - 1, 1))),
+            pltpu.SemaphoreType.DMA((units, max(chips - 1, 1))),
             pltpu.SemaphoreType.DMA((peers,)),
             pltpu.SemaphoreType.DMA((peers,)),
             pltpu.SemaphoreType.DMA((units, 2)),
@@ -385,12 +414,12 @@
             pltpu.SemaphoreType.DMA((units,)),
         ],
         compiler_params=pltpu.CompilerParams(
-            collective_id=0, has_side_effects=True, vmem_limit_bytes=64 << 20
+            collective_id=0, has_side_effects=True, vmem_limit_bytes=48 << 20
         ),
         cost_estimate=pl.CostEstimate(
             flops=pairs * HD * 4, bytes_accessed=4 * q.size, transcendentals=pairs
         ),
-    )(q, k, v, frames, noise, mask, gate)
+    )(*[pltpu.with_memory_space_constraint(x, pltpu.HBM) for x in (q, k, v, frames, noise, mask, gate)])
 
 
 def solution(mesh):

time: 34.1 us -> 31 us (0.909)
  Pallas kernels: 31.9 us -> 30 us
  local copies, waits for them, and re-layouts: 2.06 us -> 0.88 us
    pallas_call x1, Pallas kernels: 31.9 us -> 30 us  [body(): pl.pallas_call(functools.partial(kernel, levels, peers, units), out_shape...]
    unnamed x1, local copies, waits for them, and re-layouts: 2.06 us -> 0.88 us
where the time goes in v6:
time: 31 us; the launch traced here: 30.9 us
  Pallas kernels  30 us (97%)
  local copies, waits for them, and re-layouts  0.88 us (3%)
    pallas_call x1, Pallas kernels, body(): pl.pallas_call(functools.partial(kernel, levels, peers, units), out_shape...  30 us
    unnamed x1, local copies, waits for them, and re-layouts  0.88 us

profile of v6, /device:TPU:25, one launch (start us, length us, event | category | flops | bytes accessed | tf_op | source)
XLA Modules:
  0.0 30.9 jit_solution(10436835775280193644)
XLA Ops:
  0.0 30.0 %shard_map.73 = bf16[64,6144]{1,0:T(8,128)(2,1)S(1)} custom-call(bf16[64,6144]{1,0:T(8,128)(2,1)} %q_hbm.1, bf16[64,1024]{1,0:T(8,128)(2,1)} %k_hbm.1, bf16[64,1024]{1,0:T(8,128)(2,1)} %v_hbm.1, s32[8]{0:T(128)} %frames_hbm.1, s32[8]{0:T(128)} %noise_hbm.1, s32[8,8]{1,0:T(8,128)} %mask_hbm.1, bf16[64,1536]{1,0:T(8,128)(2,1)} %gate_hbm.1), custom_call_target="tpu_custom_call" | custom-call | flops 1610612736 | bytes 1572864 | tf_op jit(solution)/shard_map/pallas_call | solution.py:384
  30.0 0.9 %copy.9 = bf16[64,6144]{1,0:T(8,128)(2,1)} copy(bf16[64,6144]{1,0:T(8,128)(2,1)S(1)} %shard_map.73) | data formatting | bytes 1572864

commit v7 on v6

--- a/solution.py
+++ b/solution.py
@@ -374,7 +374,7 @@
     kv_heads = kv_width // HD // CORES
     group_rows = q.shape[1] // kv_width * rows * CORES
     chips = peers // CORES
-    units = kv_heads // 2
+    units = kv_heads
     level_spans = peers * rows // CT
     gate_rows = -(-(gate.shape[1] // HD) // 8) * 8
     hbm = pl.BlockSpec(memory_space=pltpu.HBM)

time: 31 us -> 31.3 us (level)
    pallas_call x1, Pallas kernels: 30 us -> 30.3 us  [body(): pl.pallas_call(functools.partial(kernel, levels, peers, units), out_shape...]
where the time goes in v7:
time: 31.3 us; the launch traced here: 31.2 us
  Pallas kernels  30.3 us (97%)
  local copies, waits for them, and re-layouts  0.88 us (3%)
    pallas_call x1, Pallas kernels, body(): pl.pallas_call(functools.partial(kernel, levels, peers, units), out_shape...  30.3 us
    unnamed x1, local copies, waits for them, and re-layouts  0.88 us

profile of v7, /device:TPU:25, one launch (start us, length us, event | category | flops | bytes accessed | tf_op | source)
XLA Modules:
  0.0 31.2 jit_solution(13285900240346050463)
XLA Ops:
  0.0 30.3 %shard_map.73 = bf16[64,6144]{1,0:T(8,128)(2,1)S(1)} custom-call(bf16[64,6144]{1,0:T(8,128)(2,1)} %q_hbm.1, bf16[64,1024]{1,0:T(8,128)(2,1)} %k_hbm.1, bf16[64,1024]{1,0:T(8,128)(2,1)} %v_hbm.1, s32[8]{0:T(128)} %frames_hbm.1, s32[8]{0:T(128)} %noise_hbm.1, s32[8,8]{1,0:T(8,128)} %mask_hbm.1, bf16[64,1536]{1,0:T(8,128)(2,1)} %gate_hbm.1), custom_call_target="tpu_custom_call" | custom-call | flops 1610612736 | bytes 1572864 | tf_op jit(solution)/shard_map/pallas_call | solution.py:384
  30.3 0.9 %copy.9 = bf16[64,6144]{1,0:T(8,128)(2,1)} copy(bf16[64,6144]{1,0:T(8,128)(2,1)S(1)} %shard_map.73) | data formatting | bytes 1572864

commit v8 on v7

--- a/solution.py
+++ b/solution.py
@@ -12,6 +12,7 @@
 FRAME_TOK = 32
 CT = 128
 CORES = 2
+FLIGHT = 2
 MESH = pl.DeviceIdType.MESH
 LOW = -1e30
 
@@ -183,17 +184,19 @@
             gate_send.at[step], gate_recv.at[me], {"head": target},
         )
 
-    for u in range(units):
+    def first_hop(unit, action):
         for turn in range(2):
             @pl.when(z < levels - 1)
             def _():
-                for one in first_up(u, turn):
-                    one.start()
-
-            for one in first_copies(u, turn):
-                one.start()
-        if u == 0:
-            swap.start()
+                for one in first_up(unit, turn):
+                    action(one)
+
+            for one in first_copies(unit, turn):
+                action(one)
+
+    for u in range(min(FLIGHT, units)):
+        first_hop(u, lambda one: one.start())
+    swap.start()
 
     acc[...] = jnp.zeros_like(acc)
     top[...] = jnp.full_like(top, LOW)
@@ -213,6 +216,9 @@
     token = chip * chip_rows
     span = z * level_spans + token // CT
     gate_in[me] = gate_out[token // CT]
+    for u in range(FLIGHT, units):
+        first_hop(u - FLIGHT, lambda one: one.wait_send())
+        first_hop(u, lambda one: one.start())
     for load in own:
         load.wait()
     send(
@@ -327,15 +333,8 @@
 
     lax.fori_loop(0, z + 1, one_level, 0)
 
-    for u in range(units):
-        for turn in range(2):
-            @pl.when(z < levels - 1)
-            def _():
-                for one in first_up(u, turn):
-                    one.wait_send()
-
-            for one in first_copies(u, turn):
-                one.wait_send()
+    for u in range(max(units - FLIGHT, 0), units):
+        first_hop(u, lambda one: one.wait_send())
 
     def drain(s, carry):
         level = z - s

time: 31.3 us -> 28.9 us (0.923)
  Pallas kernels: 30.3 us -> 27.8 us
    pallas_call x1, Pallas kernels: 30.3 us -> 27.8 us  [body(): pl.pallas_call(functools.partial(kernel, levels, peers, units), out_shape...]
where the time goes in v8:
time: 28.9 us; the launch traced here: 28.7 us
  Pallas kernels  27.8 us (96%)
  local copies, waits for them, and re-layouts  0.88 us (3%)
    pallas_call x1, Pallas kernels, body(): pl.pallas_call(functools.partial(kernel, levels, peers, units), out_shape...  27.8 us
    unnamed x1, local copies, waits for them, and re-layouts  0.88 us

profile of v8, /device:TPU:25, one launch (start us, length us, event | category | flops | bytes accessed | tf_op | source)
XLA Modules:
  0.0 28.7 jit_solution(12793040613367316073)
XLA Ops:
  0.0 27.8 %shard_map.73 = bf16[64,6144]{1,0:T(8,128)(2,1)S(1)} custom-call(bf16[64,6144]{1,0:T(8,128)(2,1)} %q_hbm.1, bf16[64,1024]{1,0:T(8,128)(2,1)} %k_hbm.1, bf16[64,1024]{1,0:T(8,128)(2,1)} %v_hbm.1, s32[8]{0:T(128)} %frames_hbm.1, s32[8]{0:T(128)} %noise_hbm.1, s32[8,8]{1,0:T(8,128)} %mask_hbm.1, bf16[64,1536]{1,0:T(8,128)(2,1)} %gate_hbm.1), custom_call_target="tpu_custom_call" | custom-call | flops 1610612736 | bytes 1572864 | tf_op jit(solution)/shard_map/pallas_call | solution.py:383
  27.8 0.9 %copy.9 = bf16[64,6144]{1,0:T(8,128)(2,1)} copy(bf16[64,6144]{1,0:T(8,128)(2,1)S(1)} %shard_map.73) | data formatting | bytes 1572864

commit v9 on v8

--- a/solution.py
+++ b/solution.py
@@ -308,10 +308,12 @@
     def one_level(s, carry):
         level = z - s
         for u in range(units):
-            @pl.when(s < z)
-            def _():
-                wait_slot(level - 1, u, chip)
-                issue(level - 1, u)
+            ahead, ahead_unit = 1 + (u + 1) // units, (u + 1) % units
+
+            @pl.when(s + ahead <= z)
+            def _():
+                wait_slot(level - ahead, ahead_unit, chip)
+                issue(level - ahead, ahead_unit)
 
             @pl.when(s == 0)
             def _():
@@ -330,6 +332,11 @@
             def _():
                 finish(u)
         return carry
+
+    @pl.when(z > 0)
+    def _():
+        wait_slot(z - 1, 0, chip)
+        issue(z - 1, 0)
 
     lax.fori_loop(0, z + 1, one_level, 0)
 

time: 28.9 us -> 28.9 us (level)
  no operation moved by 1% of the time
where the time goes in v9:
time: 28.9 us; the launch traced here: 28.7 us
  Pallas kernels  27.8 us (96%)
  local copies, waits for them, and re-layouts  0.88 us (3%)
    pallas_call x1, Pallas kernels, body(): pl.pallas_call(functools.partial(kernel, levels, peers, units), out_shape...  27.8 us
    unnamed x1, local copies, waits for them, and re-layouts  0.88 us

profile of v9, /device:TPU:25, one launch (start us, length us, event | category | flops | bytes accessed | tf_op | source)
XLA Modules:
  0.0 28.7 jit_solution(1705322320701675837)
XLA Ops:
  0.0 27.8 %shard_map.73 = bf16[64,6144]{1,0:T(8,128)(2,1)S(1)} custom-call(bf16[64,6144]{1,0:T(8,128)(2,1)} %q_hbm.1, bf16[64,1024]{1,0:T(8,128)(2,1)} %k_hbm.1, bf16[64,1024]{1,0:T(8,128)(2,1)} %v_hbm.1, s32[8]{0:T(128)} %frames_hbm.1, s32[8]{0:T(128)} %noise_hbm.1, s32[8,8]{1,0:T(8,128)} %mask_hbm.1, bf16[64,1536]{1,0:T(8,128)(2,1)} %gate_hbm.1), custom_call_target="tpu_custom_call" | custom-call | flops 1610612736 | bytes 1572864 | tf_op jit(solution)/shard_map/pallas_call | solution.py:390
  27.8 0.9 %copy.9 = bf16[64,6144]{1,0:T(8,128)(2,1)} copy(bf16[64,6144]{1,0:T(8,128)(2,1)S(1)} %shard_map.73) | data formatting | bytes 1572864

commit v10 on v8

--- a/solution.py
+++ b/solution.py
@@ -168,10 +168,9 @@
         def _():
             up(level, unit).start()
 
-        @pl.when(goes_across(level, unit))
-        def _():
-            for step in range(1, chips):
-                across(level, unit, step).start()
+    def start_across(level, unit):
+        for step in range(1, chips):
+            across(level, unit, step).start()
 
     swap = send(
         half(q_hbm, 1 - core), q_ref.at[core], q_send.at[0], q_recv.at[0], {"head": sibling}
@@ -324,6 +323,22 @@
                 def _():
                     for step in range(1, chips):
                         up_other(u, step).start()
+            turn, later = (u + FLIGHT) // units, (u + FLIGHT) % units
+
+            @pl.when((s + turn >= 1) & (s + turn <= z))
+            def _():
+                if chips != 2:
+                    start_across(level - turn, later)
+                else:
+                    @pl.when(level - turn > 0)
+                    def _():
+                        start_across(level - turn, later)
+
+                    early = later + later % 2
+                    if early < units and (later == 0 or later % 2 == 1):
+                        @pl.when(level - turn == 0)
+                        def _():
+                            start_across(level - turn, early)
             fold(level, u)
 
             @pl.when(s == z)

time: 28.9 us -> 33.4 us (1.16)
  Pallas kernels: 27.8 us -> 32.4 us
    pallas_call x1, Pallas kernels: 27.8 us -> 32.4 us  [body(): pl.pallas_call(functools.partial(kernel, levels, peers, units), out_shape...]
where the time goes in v10:
time: 33.4 us; the launch traced here: 33.3 us
  Pallas kernels  32.4 us (97%)
  local copies, waits for them, and re-layouts  0.88 us (3%)
    pallas_call x1, Pallas kernels, body(): pl.pallas_call(functools.partial(kernel, levels, peers, units), out_shape...  32.4 us
    unnamed x1, local copies, waits for them, and re-layouts  0.88 us

profile of v10, /device:TPU:25, one launch (start us, length us, event | category | flops | bytes accessed | tf_op | source)
XLA Modules:
  0.0 33.3 jit_solution(14843210962423261771)
XLA Ops:
  0.0 32.4 %shard_map.73 = bf16[64,6144]{1,0:T(8,128)(2,1)S(1)} custom-call(bf16[64,6144]{1,0:T(8,128)(2,1)} %q_hbm.1, bf16[64,1024]{1,0:T(8,128)(2,1)} %k_hbm.1, bf16[64,1024]{1,0:T(8,128)(2,1)} %v_hbm.1, s32[8]{0:T(128)} %frames_hbm.1, s32[8]{0:T(128)} %noise_hbm.1, s32[8,8]{1,0:T(8,128)} %mask_hbm.1, bf16[64,1536]{1,0:T(8,128)(2,1)} %gate_hbm.1), custom_call_target="tpu_custom_call" | custom-call | flops 1610612736 | bytes 1572864 | tf_op jit(solution)/shard_map/pallas_call | solution.py:398
  32.4 0.9 %copy.9 = bf16[64,6144]{1,0:T(8,128)(2,1)} copy(bf16[64,6144]{1,0:T(8,128)(2,1)S(1)} %shard_map.73) | data formatting | bytes 1572864

commit v11 on v8

--- a/solution.py
+++ b/solution.py
@@ -12,7 +12,7 @@
 FRAME_TOK = 32
 CT = 128
 CORES = 2
-FLIGHT = 2
+FLIGHT = 3
 MESH = pl.DeviceIdType.MESH
 LOW = -1e30
 

time: 28.9 us -> 30.3 us (1.048)
  Pallas kernels: 27.8 us -> 29.2 us
    pallas_call x1, Pallas kernels: 27.8 us -> 29.2 us  [body(): pl.pallas_call(functools.partial(kernel, levels, peers, units), out_shape...]
where the time goes in v11:
time: 30.3 us; the launch traced here: 30.1 us
  Pallas kernels  29.2 us (96%)
  local copies, waits for them, and re-layouts  0.88 us (3%)
    pallas_call x1, Pallas kernels, body(): pl.pallas_call(functools.partial(kernel, levels, peers, units), out_shape...  29.2 us
    unnamed x1, local copies, waits for them, and re-layouts  0.88 us

profile of v11, /device:TPU:25, one launch (start us, length us, event | category | flops | bytes accessed | tf_op | source)
XLA Modules:
  0.0 30.1 jit_solution(18260709375411967591)
XLA Ops:
  0.0 29.2 %shard_map.73 = bf16[64,6144]{1,0:T(8,128)(2,1)S(1)} custom-call(bf16[64,6144]{1,0:T(8,128)(2,1)} %q_hbm.1, bf16[64,1024]{1,0:T(8,128)(2,1)} %k_hbm.1, bf16[64,1024]{1,0:T(8,128)(2,1)} %v_hbm.1, s32[8]{0:T(128)} %frames_hbm.1, s32[8]{0:T(128)} %noise_hbm.1, s32[8,8]{1,0:T(8,128)} %mask_hbm.1, bf16[64,1536]{1,0:T(8,128)(2,1)} %gate_hbm.1), custom_call_target="tpu_custom_call" | custom-call | flops 1610612736 | bytes 1572864 | tf_op jit(solution)/shard_map/pallas_call | solution.py:383
  29.2 0.9 %copy.9 = bf16[64,6144]{1,0:T(8,128)(2,1)} copy(bf16[64,6144]{1,0:T(8,128)(2,1)S(1)} %shard_map.73) | data formatting | bytes 1572864
